TPU v7x, 32 devices: a whole 2x2x4 slice. The times are simulated.
32 devices in a mesh: src: 4 (over z), tgt: 8 (over y, x, core).
Axes of the slice: x: 2, y: 2, z: 4, core: 2. Of those that a mesh axis runs over, the one named last changes fastest.
Arguments:
- generator: int32 [64], replicated, may hold values from 1 to 8191, as said below
- shift: float32 [64], replicated, may hold values from 0 to 1
- targets: float32 [64, 8192], P(None, 'tgt'), may hold values from -8 to 8
- log_weights: float32 [8192], P('tgt'), may hold values from -20 to 150
Outputs:
- potential_f: float32 [8192], P('src')
- potential_g: float32 [8192], P('tgt')
Inputs may be any that keep to these rules, and one draw needn't show every extreme that they name: `generator`: odd integers.
All inputs are finite; a program needn't handle non-finite values.
Results may differ from a plain program's by a relative error of at most 0.0003.
Values sent between devices are 32-bit elements; how exact they have to be, the bound alone decides.
A program may use at most 64 MiB of HBM per device.

v0:
```python
import jax
import jax.numpy as jnp
from jax import lax
from jax.sharding import PartitionSpec as P

SRC_DEV = 2048
ITERS = 2


blur_level = 0.1
highest = lax.Precision.HIGHEST


def lattice_block(generator, shift, start, count, modulus):
    index = start + jnp.arange(count, dtype=jnp.int32)
    folded = index[None, :] * generator[:, None] % modulus
    phase = folded.astype(jnp.float32) / modulus + shift[:, None]
    return jnp.sin(2.0 * jnp.pi * phase)


def cost_block(points, targets, far):
    cross = lax.dot_general(
        points,
        targets,
        (((0,), (0,)), ((), ())),
        precision=highest,
        preferred_element_type=jnp.float32,
    )
    near = 0.5 * jnp.sum(points * points, 0)
    return near[:, None] + far[None, :] - cross


def weight_reduce(peak, total):
    top = lax.pmax(peak, "tgt")
    return (top, lax.psum(total * jnp.exp(peak - top), "tgt"))


def row_reduce(peak, total):
    peaks, totals = (
        lax.all_to_all(peak[None, :], "tgt", split_axis=1, concat_axis=0, tiled=True),
        lax.all_to_all(total[None, :], "tgt", split_axis=1, concat_axis=0, tiled=True),
    )
    top = jnp.max(peaks, 0)
    summed = jnp.sum(totals * jnp.exp(peaks - top[None, :]), 0)
    share = -blur_level * (top + jnp.log(summed))
    return lax.all_gather(share, "tgt", axis=0, tiled=True)


def column_reduce(peak, total):
    top = lax.pmax(peak, "src")
    summed = lax.psum(total * jnp.exp(peak - top), "src")
    return -blur_level * (top + jnp.log(summed))


def local(generator, shift, targets, log_weights):
    modulus = SRC_DEV * lax.axis_size("src")
    offset = lax.axis_index("src") * SRC_DEV
    block = min(512, SRC_DEV)
    count = SRC_DEV // block
    local_peak = jnp.max(log_weights)
    local_total = jnp.sum(jnp.exp(log_weights - local_peak))
    weight_top, weight_sum = weight_reduce(local_peak, local_total)
    log_b = log_weights - (weight_top + jnp.log(weight_sum))
    log_a = -jnp.log(jnp.float32(modulus))
    far = 0.5 * jnp.sum(targets * targets, 0)
    columns = targets.shape[1]
    potential_g = jnp.zeros((columns,), jnp.float32)
    potential_f = jnp.zeros((SRC_DEV,), jnp.float32)
    for step in range(ITERS):

        def row_pass(index, current_g=potential_g):
            points = lattice_block(generator, shift, offset + index * block, block, modulus)
            scores = (
                log_b[None, :]
                + (current_g[None, :] - cost_block(points, targets, far)) / blur_level
            )
            top = jnp.max(scores, 1)
            return (top, jnp.sum(jnp.exp(scores - top[:, None]), 1))

        peaks, totals = lax.map(row_pass, jnp.arange(count, dtype=jnp.int32))
        potential_f = row_reduce(peaks.reshape(SRC_DEV), totals.reshape(SRC_DEV))

        def column_pass(carry, index, current_f=potential_f):
            peak_c, total_c = carry
            start = index * block
            points = lattice_block(generator, shift, offset + start, block, modulus)
            part = lax.dynamic_slice_in_dim(current_f, start, block)
            scores = log_a + (part[:, None] - cost_block(points, targets, far)) / blur_level
            top = jnp.maximum(peak_c, jnp.max(scores, 0))
            total = total_c * jnp.exp(peak_c - top) + jnp.sum(jnp.exp(scores - top[None, :]), 0)
            return ((top, total), None)

        start_carry = (jnp.full((columns,), -1e30, jnp.float32), jnp.zeros((columns,), jnp.float32))
        (top, total), unused = lax.scan(
            column_pass, start_carry, jnp.arange(count, dtype=jnp.int32)
        )
        potential_g = column_reduce(top, total)
    return (potential_f, potential_g)


def solution(mesh):
    in_specs = (P(), P(), P(None, "tgt"), P("tgt"))
    out_specs = (P("src"), P("tgt"))
    return jax.shard_map(local, mesh=mesh, in_specs=in_specs, out_specs=out_specs, check_vma=False)
```

profile of v0, /device:TPU:0, one launch (start us, length us, event | category | flops | bytes accessed | tf_op | source)
XLA Modules:
  0.0 236.1 jit_solution(2660378012309222714)
XLA Ops:
  0.6 1.3 reduce_max.75
  1.9 15.7 %pmax.21 = f32[]{:T(128)} all-reduce(f32[]{:T(128)} %reduce_max.75), channel_id=1, replica_groups=mesh['src'=4,'tgt'=8] {'tgt'}, use_global_device_ids=true, to_apply=%region_1.0 | all-reduce | flops 1 | bytes 8 | tf_op jit(solution)/shard_map/pmax | solution.py:34
  17.7 2.0 exponential_reduce_fusion.4
  21.7 12.3 %psum.21 = f32[]{:T(128)} all-reduce(f32[]{:T(128)S(6)} %mul.267), channel_id=1, replica_groups=mesh['src'=4,'tgt'=8] {'tgt'}, use_global_device_ids=true, to_apply=%region_3.0 | all-reduce | flops 1 | bytes 8 | tf_op jit(solution)/shard_map/psum | solution.py:35
  35.4 0.7 broadcast_subtract_fusion
  36.0 1.0 multiply_reduce_fusion.4
  37.1 27.8 %while.58 = (s32[]{:T(128)}, f32[4,512]{1,0:T(4,128)S(1)}, f32[4,512]{1,0:T(4,128)S(1)}, f32[1024]{0:T(1024)S(1)}, s32[4]{0:T(128)S(1)}, /*index=5*/s32[]{:T(128...) while((s32[]{:T(128)}, f32[4,512]{1,0:T(4,128)S(1)}, ...), condition=%wide.region_9.10_spmd, body=%wide.region_5.9_spmd.sunk | while | flops 407961088 | bytes 4494509 | solution.py:80
  38.3 1.3 multiply_reduce_fusion.9
  39.6 3.8 %fusion.75 = (f32[512]{0:T(512)S(1)}, f32[512,1024]{1,0:T(8,128)S(1)}) fusion(f32[64,1024]{1,0:T(8,128)} %get-tuple-element.987, f32[64]{0:T(128)} %get-tuple-element.985, s32[64]{0:T(128)} %get-tuple-element.984, s32[512]{0:T(512)S(1)} %iota_add_fusion.8, f32[1024]{0:T(1024)S(1)} %get-tuple-element.986, f32[512]{0:T(512)S(1)} %broadcast_multiply_fusion.9, ...), kind=kOutput, calls=%fused_computation.108.clone.1 | convolution fusion | flops 406322688 | bytes 2374144 | tf_op jit(solution)/shard_map/while/body/eval_jaxpr/dot_general | solution.py:22
  45.3 1.3 multiply_reduce_fusion.9
  46.6 3.8 %fusion.75 = (f32[512]{0:T(512)S(1)}, f32[512,1024]{1,0:T(8,128)S(1)}) fusion(f32[64,1024]{1,0:T(8,128)} %get-tuple-element.987, f32[64]{0:T(128)} %get-tuple-element.985, s32[64]{0:T(128)} %get-tuple-element.984, s32[512]{0:T(512)S(1)} %iota_add_fusion.8, f32[1024]{0:T(1024)S(1)} %get-tuple-element.986, f32[512]{0:T(512)S(1)} %broadcast_multiply_fusion.9, ...), kind=kOutput, calls=%fused_computation.108.clone.1 | convolution fusion | flops 406322688 | bytes 2374144 | tf_op jit(solution)/shard_map/while/body/eval_jaxpr/dot_general | solution.py:22
  52.2 1.3 multiply_reduce_fusion.9
  53.5 3.8 %fusion.75 = (f32[512]{0:T(512)S(1)}, f32[512,1024]{1,0:T(8,128)S(1)}) fusion(f32[64,1024]{1,0:T(8,128)} %get-tuple-element.987, f32[64]{0:T(128)} %get-tuple-element.985, s32[64]{0:T(128)} %get-tuple-element.984, s32[512]{0:T(512)S(1)} %iota_add_fusion.8, f32[1024]{0:T(1024)S(1)} %get-tuple-element.986, f32[512]{0:T(512)S(1)} %broadcast_multiply_fusion.9, ...), kind=kOutput, calls=%fused_computation.108.clone.1 | convolution fusion | flops 406322688 | bytes 2374144 | tf_op jit(solution)/shard_map/while/body/eval_jaxpr/dot_general | solution.py:22
  59.2 1.3 multiply_reduce_fusion.9
  60.5 3.8 %fusion.75 = (f32[512]{0:T(512)S(1)}, f32[512,1024]{1,0:T(8,128)S(1)}) fusion(f32[64,1024]{1,0:T(8,128)} %get-tuple-element.987, f32[64]{0:T(128)} %get-tuple-element.985, s32[64]{0:T(128)} %get-tuple-element.984, s32[512]{0:T(512)S(1)} %iota_add_fusion.8, f32[1024]{0:T(1024)S(1)} %get-tuple-element.986, f32[512]{0:T(512)S(1)} %broadcast_multiply_fusion.9, ...), kind=kOutput, calls=%fused_computation.108.clone.1 | convolution fusion | flops 406322688 | bytes 2374144 | tf_op jit(solution)/shard_map/while/body/eval_jaxpr/dot_general | solution.py:22
  64.8 0.6 all_to_all.48
  65.5 3.3 %all-to-all-start = ((f32[1,8,256]{2,0,1:T(1,128)}), f32[1,8,256]{2,0,1:T(1,128)S(1)}, u32[]{:S(2)}, u32[]{:S(2)}) async-start(f32[1,8,256]{2,0,1:T(1,128)} %all_to_all.48), calls=%async_computation | async-start | bytes 16384 | tf_op jit(solution)/shard_map/all_to_all | solution.py:40
  68.8 0.6 all_to_all.50
  69.4 4.0 %all-to-all-done = f32[1,8,256]{2,0,1:T(1,128)S(1)} async-done(((f32[1,8,256]{2,0,1:T(1,128)}), f32[1,8,256]{2,0,1:T(1,128)S(1)}, u32[]{:S(2)}, u32[]{:S(2)}) %all-to-all-start) | async-done | bytes 8224 | tf_op jit(solution)/shard_map/all_to_all | solution.py:40
  73.4 3.3 %all-to-all-start.1 = ((f32[1,8,256]{2,0,1:T(1,128)}), f32[1,8,256]{2,0,1:T(1,128)S(1)}, u32[]{:S(2)}, u32[]{:S(2)}) async-start(f32[1,8,256]{2,0,1:T(1,128)} %all_to_all.50), calls=%async_computation.1 | async-start | bytes 16384 | tf_op jit(solution)/shard_map/all_to_all | solution.py:41
  76.8 4.6 %all-to-all-done.1 = f32[1,8,256]{2,0,1:T(1,128)S(1)} async-done(((f32[1,8,256]{2,0,1:T(1,128)}), f32[1,8,256]{2,0,1:T(1,128)S(1)}, u32[]{:S(2)}, u32[]{:S(2)}) %all-to-all-start.1) | async-done | bytes 8224 | tf_op jit(solution)/shard_map/all_to_all | solution.py:41
  81.5 7.9 %all-gather = f32[8,1,256]{2,1,0:T(1,128)S(1)} all-gather(f32[1,1,256]{2,1,0:T(1,128)S(1)} %bitcast.66), channel_id=1, replica_groups=mesh['src'=4,'tgt'=8] {'tgt'}, dimensions={0}, use_global_device_ids=true | all-gather | bytes 9216 | tf_op jit(solution)/shard_map/all_gather | solution.py:46
  89.4 27.2 %while.60 = (s32[]{:T(128)}, f32[1024]{0:T(1024)S(1)}, f32[1024]{0:T(1024)S(1)}, s32[4]{0:T(128)S(1)}, f32[2048]{0:T(1024)S(1)}, /*index=5*/s32[]{:T(128)}, s32[...) while((s32[]{:T(128)}, f32[1024]{0:T(1024)S(1)}, ...), condition=%wide.region_16.17_spmd.clone, body=%wide.region_12.16_spmd.clone.sunk | while | flops 407967232 | bytes 4535518 | solution.py:94
  89.4 0.7 dynamic_slice.49
  90.9 1.3 multiply_reduce_fusion.11
  92.1 3.7 %fusion.79 = (f32[1024]{0:T(1024)S(1)}, f32[512,1024]{1,0:T(8,128)S(1)}) fusion(f32[64,1024]{1,0:T(8,128)} %get-tuple-element.1028, f32[64]{0:T(128)} %get-tuple-element.1026, s32[64]{0:T(128)} %get-tuple-element.1025, s32[512]{0:T(512)S(1)} %iota_add_fusion.10, f32[1024]{0:T(1024)S(1)} %get-tuple-element.1027, ...), kind=kOutput, calls=%fused_computation.110.clone.1 | convolution fusion | flops 406322176 | bytes 2374144 | tf_op jit(solution)/shard_map/while/body/eval_jaxpr/dot_general | solution.py:22
  96.2 0.7 dynamic_slice.49
  97.7 1.3 multiply_reduce_fusion.11
  99.0 3.7 %fusion.79 = (f32[1024]{0:T(1024)S(1)}, f32[512,1024]{1,0:T(8,128)S(1)}) fusion(f32[64,1024]{1,0:T(8,128)} %get-tuple-element.1028, f32[64]{0:T(128)} %get-tuple-element.1026, s32[64]{0:T(128)} %get-tuple-element.1025, s32[512]{0:T(512)S(1)} %iota_add_fusion.10, f32[1024]{0:T(1024)S(1)} %get-tuple-element.1027, ...), kind=kOutput, calls=%fused_computation.110.clone.1 | convolution fusion | flops 406322176 | bytes 2374144 | tf_op jit(solution)/shard_map/while/body/eval_jaxpr/dot_general | solution.py:22
  103.0 0.7 dynamic_slice.49
  104.5 1.3 multiply_reduce_fusion.11
  105.8 3.7 %fusion.79 = (f32[1024]{0:T(1024)S(1)}, f32[512,1024]{1,0:T(8,128)S(1)}) fusion(f32[64,1024]{1,0:T(8,128)} %get-tuple-element.1028, f32[64]{0:T(128)} %get-tuple-element.1026, s32[64]{0:T(128)} %get-tuple-element.1025, s32[512]{0:T(512)S(1)} %iota_add_fusion.10, f32[1024]{0:T(1024)S(1)} %get-tuple-element.1027, ...), kind=kOutput, calls=%fused_computation.110.clone.1 | convolution fusion | flops 406322176 | bytes 2374144 | tf_op jit(solution)/shard_map/while/body/eval_jaxpr/dot_general | solution.py:22
  109.8 0.7 dynamic_slice.49
  111.3 1.3 multiply_reduce_fusion.11
  112.6 3.7 %fusion.79 = (f32[1024]{0:T(1024)S(1)}, f32[512,1024]{1,0:T(8,128)S(1)}) fusion(f32[64,1024]{1,0:T(8,128)} %get-tuple-element.1028, f32[64]{0:T(128)} %get-tuple-element.1026, s32[64]{0:T(128)} %get-tuple-element.1025, s32[512]{0:T(512)S(1)} %iota_add_fusion.10, f32[1024]{0:T(1024)S(1)} %get-tuple-element.1027, ...), kind=kOutput, calls=%fused_computation.110.clone.1 | convolution fusion | flops 406322176 | bytes 2374144 | tf_op jit(solution)/shard_map/while/body/eval_jaxpr/dot_general | solution.py:22
  116.7 12.0 %pmax.22 = f32[1024]{0:T(1024)S(1)} all-reduce(f32[1024]{0:T(1024)S(1)} %get-tuple-element.524), channel_id=1, replica_groups=mesh['src'=4,'tgt'=8] {'src'}, use_global_device_ids=true, to_apply=%region_17.18 | all-reduce | flops 1024 | bytes 8192 | tf_op jit(solution)/shard_map/pmax | solution.py:50
  128.6 8.4 %psum.22 = f32[1024]{0:T(1024)S(1)} all-reduce(f32[1024]{0:T(1024)S(1)} %exponential_multiply_fusion.1), channel_id=1, replica_groups=mesh['src'=4,'tgt'=8] {'src'}, use_global_device_ids=true, to_apply=%region_18.19 | all-reduce | flops 1024 | bytes 8192 | tf_op jit(solution)/shard_map/psum | solution.py:51
  137.0 27.8 %while.59 = (s32[]{:T(128)}, f32[4,512]{1,0:T(4,128)S(1)}, f32[4,512]{1,0:T(4,128)S(1)}, f32[1024]{0:T(1024)S(1)}, f32[1024]{0:T(1024)S(1)}, /*index=5*/s32[4]{0...) while((s32[]{:T(128)}, f32[4,512]{1,0:T(4,128)S(1)}, ...), condition=%wide.region_23.24_spmd, body=%wide.region_19.23_spmd.sunk | while | flops 407961088 | bytes 4498613 | solution.py:80
  138.3 1.3 multiply_reduce_fusion.10
  139.6 3.8 %fusion.77 = (f32[512]{0:T(512)S(1)}, f32[512,1024]{1,0:T(8,128)S(1)}) fusion(f32[64,1024]{1,0:T(8,128)} %get-tuple-element.1071, f32[64]{0:T(128)} %get-tuple-element.1069, s32[64]{0:T(128)} %get-tuple-element.1068, s32[512]{0:T(512)S(1)} %iota_add_fusion.9, f32[1024]{0:T(1024)S(1)} %get-tuple-element.1070, f32[512]{0:T(512)S(1)} %broadcast_multiply_fusion.10, ...), kind=kOutput, calls=%fused_computation.109.clone.1 | convolution fusion | flops 406322688 | bytes 2378240 | tf_op jit(solution)/shard_map/while/body/eval_jaxpr/dot_general | solution.py:22
  145.2 1.3 multiply_reduce_fusion.10
  146.5 3.8 %fusion.77 = (f32[512]{0:T(512)S(1)}, f32[512,1024]{1,0:T(8,128)S(1)}) fusion(f32[64,1024]{1,0:T(8,128)} %get-tuple-element.1071, f32[64]{0:T(128)} %get-tuple-element.1069, s32[64]{0:T(128)} %get-tuple-element.1068, s32[512]{0:T(512)S(1)} %iota_add_fusion.9, f32[1024]{0:T(1024)S(1)} %get-tuple-element.1070, f32[512]{0:T(512)S(1)} %broadcast_multiply_fusion.10, ...), kind=kOutput, calls=%fused_computation.109.clone.1 | convolution fusion | flops 406322688 | bytes 2378240 | tf_op jit(solution)/shard_map/while/body/eval_jaxpr/dot_general | solution.py:22
  152.2 1.3 multiply_reduce_fusion.10
  153.5 3.8 %fusion.77 = (f32[512]{0:T(512)S(1)}, f32[512,1024]{1,0:T(8,128)S(1)}) fusion(f32[64,1024]{1,0:T(8,128)} %get-tuple-element.1071, f32[64]{0:T(128)} %get-tuple-element.1069, s32[64]{0:T(128)} %get-tuple-element.1068, s32[512]{0:T(512)S(1)} %iota_add_fusion.9, f32[1024]{0:T(1024)S(1)} %get-tuple-element.1070, f32[512]{0:T(512)S(1)} %broadcast_multiply_fusion.10, ...), kind=kOutput, calls=%fused_computation.109.clone.1 | convolution fusion | flops 406322688 | bytes 2378240 | tf_op jit(solution)/shard_map/while/body/eval_jaxpr/dot_general | solution.py:22
  159.1 1.3 multiply_reduce_fusion.10
  160.4 3.8 %fusion.77 = (f32[512]{0:T(512)S(1)}, f32[512,1024]{1,0:T(8,128)S(1)}) fusion(f32[64,1024]{1,0:T(8,128)} %get-tuple-element.1071, f32[64]{0:T(128)} %get-tuple-element.1069, s32[64]{0:T(128)} %get-tuple-element.1068, s32[512]{0:T(512)S(1)} %iota_add_fusion.9, f32[1024]{0:T(1024)S(1)} %get-tuple-element.1070, f32[512]{0:T(512)S(1)} %broadcast_multiply_fusion.10, ...), kind=kOutput, calls=%fused_computation.109.clone.1 | convolution fusion | flops 406322688 | bytes 2378240 | tf_op jit(solution)/shard_map/while/body/eval_jaxpr/dot_general | solution.py:22
  164.8 0.6 all_to_all.54
  165.5 3.3 %all-to-all-start.2 = ((f32[1,8,256]{2,0,1:T(1,128)}), f32[1,8,256]{2,0,1:T(1,128)S(1)}, u32[]{:S(2)}, u32[]{:S(2)}) async-start(f32[1,8,256]{2,0,1:T(1,128)} %all_to_all.54), calls=%async_computation.2 | async-start | bytes 16384 | tf_op jit(solution)/shard_map/all_to_all | solution.py:40
  168.8 0.6 all_to_all.56
  169.4 4.0 %all-to-all-done.2 = f32[1,8,256]{2,0,1:T(1,128)S(1)} async-done(((f32[1,8,256]{2,0,1:T(1,128)}), f32[1,8,256]{2,0,1:T(1,128)S(1)}, u32[]{:S(2)}, u32[]{:S(2)}) %all-to-all-start.2) | async-done | bytes 8224 | tf_op jit(solution)/shard_map/all_to_all | solution.py:40
  173.4 3.3 %all-to-all-start.3 = ((f32[1,8,256]{2,0,1:T(1,128)}), f32[1,8,256]{2,0,1:T(1,128)S(1)}, u32[]{:S(2)}, u32[]{:S(2)}) async-start(f32[1,8,256]{2,0,1:T(1,128)} %all_to_all.56), calls=%async_computation.3 | async-start | bytes 16384 | tf_op jit(solution)/shard_map/all_to_all | solution.py:41
  176.8 4.6 %all-to-all-done.3 = f32[1,8,256]{2,0,1:T(1,128)S(1)} async-done(((f32[1,8,256]{2,0,1:T(1,128)}), f32[1,8,256]{2,0,1:T(1,128)S(1)}, u32[]{:S(2)}, u32[]{:S(2)}) %all-to-all-start.3) | async-done | bytes 8224 | tf_op jit(solution)/shard_map/all_to_all | solution.py:41
  181.4 7.9 %all-gather.1 = f32[8,1,256]{2,1,0:T(1,128)S(1)} all-gather(f32[1,1,256]{2,1,0:T(1,128)S(1)} %bitcast.67), channel_id=1, replica_groups=mesh['src'=4,'tgt'=8] {'tgt'}, dimensions={0}, use_global_device_ids=true | all-gather | bytes 9216 | tf_op jit(solution)/shard_map/all_gather | solution.py:46
  189.4 26.7 %while.61 = (s32[]{:T(128)}, f32[1024]{0:T(1024)S(1)}, f32[1024]{0:T(1024)S(1)}, s32[4]{0:T(128)S(1)}, f32[2048]{0:T(1024)S(1)}, /*index=5*/s32[]{:T(128)}, s32[...) while((s32[]{:T(128)}, f32[1024]{0:T(1024)S(1)}, ...), condition=%wide.region_30.31_spmd.clone, body=%wide.region_26.30_spmd.clone.sunk | while | flops 407967232 | bytes 4535518 | solution.py:94
  190.7 1.3 multiply_reduce_fusion.12
  192.0 3.7 %fusion.82 = (f32[1024]{0:T(1024)S(1)}, f32[512,1024]{1,0:T(8,128)S(1)}) fusion(f32[64,1024]{1,0:T(8,128)} %get-tuple-element.1112, f32[64]{0:T(128)} %get-tuple-element.1110, s32[64]{0:T(128)} %get-tuple-element.1109, s32[512]{0:T(512)S(1)} %iota_add_fusion.11, f32[1024]{0:T(1024)S(1)} %get-tuple-element.1111, ...), kind=kOutput, calls=%fused_computation.111.clone.1 | convolution fusion | flops 406322176 | bytes 2374144 | tf_op jit(solution)/shard_map/while/body/eval_jaxpr/dot_general | solution.py:22
  197.4 1.3 multiply_reduce_fusion.12
  198.7 3.7 %fusion.82 = (f32[1024]{0:T(1024)S(1)}, f32[512,1024]{1,0:T(8,128)S(1)}) fusion(f32[64,1024]{1,0:T(8,128)} %get-tuple-element.1112, f32[64]{0:T(128)} %get-tuple-element.1110, s32[64]{0:T(128)} %get-tuple-element.1109, s32[512]{0:T(512)S(1)} %iota_add_fusion.11, f32[1024]{0:T(1024)S(1)} %get-tuple-element.1111, ...), kind=kOutput, calls=%fused_computation.111.clone.1 | convolution fusion | flops 406322176 | bytes 2374144 | tf_op jit(solution)/shard_map/while/body/eval_jaxpr/dot_general | solution.py:22
  204.1 1.3 multiply_reduce_fusion.12
  205.4 3.7 %fusion.82 = (f32[1024]{0:T(1024)S(1)}, f32[512,1024]{1,0:T(8,128)S(1)}) fusion(f32[64,1024]{1,0:T(8,128)} %get-tuple-element.1112, f32[64]{0:T(128)} %get-tuple-element.1110, s32[64]{0:T(128)} %get-tuple-element.1109, s32[512]{0:T(512)S(1)} %iota_add_fusion.11, f32[1024]{0:T(1024)S(1)} %get-tuple-element.1111, ...), kind=kOutput, calls=%fused_computation.111.clone.1 | convolution fusion | flops 406322176 | bytes 2374144 | tf_op jit(solution)/shard_map/while/body/eval_jaxpr/dot_general | solution.py:22
  210.8 1.3 multiply_reduce_fusion.12
  212.1 3.7 %fusion.82 = (f32[1024]{0:T(1024)S(1)}, f32[512,1024]{1,0:T(8,128)S(1)}) fusion(f32[64,1024]{1,0:T(8,128)} %get-tuple-element.1112, f32[64]{0:T(128)} %get-tuple-element.1110, s32[64]{0:T(128)} %get-tuple-element.1109, s32[512]{0:T(512)S(1)} %iota_add_fusion.11, f32[1024]{0:T(1024)S(1)} %get-tuple-element.1111, ...), kind=kOutput, calls=%fused_computation.111.clone.1 | convolution fusion | flops 406322176 | bytes 2374144 | tf_op jit(solution)/shard_map/while/body/eval_jaxpr/dot_general | solution.py:22
  216.1 10.4 %pmax.23 = f32[1024]{0:T(1024)S(1)} all-reduce(f32[1024]{0:T(1024)S(1)} %get-tuple-element.528), channel_id=1, replica_groups=mesh['src'=4,'tgt'=8] {'src'}, use_global_device_ids=true, to_apply=%region_31.32 | all-reduce | flops 1024 | bytes 8192 | tf_op jit(solution)/shard_map/pmax | solution.py:50
  226.5 8.4 %psum.23 = f32[1024]{0:T(1024)S(1)} all-reduce(f32[1024]{0:T(1024)S(1)} %exponential_multiply_fusion), channel_id=1, replica_groups=mesh['src'=4,'tgt'=8] {'src'}, use_global_device_ids=true, to_apply=%region_32.33 | all-reduce | flops 1024 | bytes 8192 | tf_op jit(solution)/shard_map/psum | solution.py:51
  (132 shorter events, 16.9 us)
Async XLA Ops:
  65.5 8.0 %all-to-all-start = ((f32[1,8,256]{2,0,1:T(1,128)}), f32[1,8,256]{2,0,1:T(1,128)S(1)}, u32[]{:S(2)}, u32[]{:S(2)}) async-start(f32[1,8,256]{2,0,1:T(1,128)} %all_to_all.48), calls=%async_computation | async-start | bytes 16384 | tf_op jit(solution)/shard_map/all_to_all | solution.py:40
  73.4 8.0 %all-to-all-start.1 = ((f32[1,8,256]{2,0,1:T(1,128)}), f32[1,8,256]{2,0,1:T(1,128)S(1)}, u32[]{:S(2)}, u32[]{:S(2)}) async-start(f32[1,8,256]{2,0,1:T(1,128)} %all_to_all.50), calls=%async_computation.1 | async-start | bytes 16384 | tf_op jit(solution)/shard_map/all_to_all | solution.py:41
  165.5 8.0 %all-to-all-start.2 = ((f32[1,8,256]{2,0,1:T(1,128)}), f32[1,8,256]{2,0,1:T(1,128)S(1)}, u32[]{:S(2)}, u32[]{:S(2)}) async-start(f32[1,8,256]{2,0,1:T(1,128)} %all_to_all.54), calls=%async_computation.2 | async-start | bytes 16384 | tf_op jit(solution)/shard_map/all_to_all | solution.py:40
  173.4 8.0 %all-to-all-start.3 = ((f32[1,8,256]{2,0,1:T(1,128)}), f32[1,8,256]{2,0,1:T(1,128)S(1)}, u32[]{:S(2)}, u32[]{:S(2)}) async-start(f32[1,8,256]{2,0,1:T(1,128)} %all_to_all.56), calls=%async_computation.3 | async-start | bytes 16384 | tf_op jit(solution)/shard_map/all_to_all | solution.py:41
where the time goes:
time: 237 us; the launch traced here: 236 us
  blocking collectives  83 us (35%)
  matrix products  59.7 us (25%)
  other arithmetic  33.2 us (14%)
  waiting for transfers between devices  17.2 us (7%)
  local copies, waits for them, and re-layouts  14.2 us (6%)
  starting transfers between devices  13.3 us (6%)
  loops' own time  11.3 us (5%)
  between operations  4.18 us (2%)
    dot_general x16, matrix products, cost_block(): lax.dot_general(points, targets, (((0,), (0,)), ((), ())), precision=high...  59.7 us
    pmax x2, blocking collectives, column_reduce(): top = lax.pmax(peak, 'src')  22.3 us
    reduce_sum x16, other arithmetic, cost_block(): near = 0.5 * jnp.sum(points * points, 0)  20.4 us
    psum x2, blocking collectives, column_reduce(): summed = lax.psum(total * jnp.exp(peak - top), 'src')  16.7 us
    all_gather x2, blocking collectives, row_reduce(): return lax.all_gather(share, 'tgt', axis=0, tiled=True)  15.9 us
    pmax x1, blocking collectives, weight_reduce(): top = lax.pmax(peak, 'tgt')  15.7 us
    psum x1, blocking collectives, weight_reduce(): return (top, lax.psum(total * jnp.exp(peak - top), 'tgt'))  12.3 us
    dynamic_slice x16, local copies, waits for them, and re-layouts, local(): peaks, totals = lax.map(row_pass, jnp.arange(count, dtype=jnp.int32))  9.7 us
  transfers between devices with their start and end apart: 4, of which 4 were waited for; matrix products, arithmetic and copies ran while one was open for 0% of the time, Pallas kernels for 0%

commit v1 on v0

v1 whole, which is shorter than its diff:
```python
import functools
import math

import jax
import jax.numpy as jnp
from jax import lax
from jax.experimental import pallas as pl
from jax.experimental.pallas import tpu as pltpu
from jax.sharding import PartitionSpec as P

SRC_DEV = 2048
ITERS = 2
LANES = 128
WIDE = 256

blur_level = 0.1
log2_e = math.log2(math.e)
scale = log2_e / blur_level
MESH = pl.DeviceIdType.MESH
f32 = jnp.float32
bf16 = jnp.bfloat16


def sine_cosine(turns):
    half = (turns - jnp.round(turns)) * f32(math.pi)
    square = half * half
    sine = f32(1.0 / math.factorial(13))
    cosine = f32(1.0 / math.factorial(12))
    for order in (11, 9, 7, 5, 3, 1):
        sign = -1.0 if (order // 2) % 2 else 1.0
        sine = sine * square + f32(sign / math.factorial(order))
    for order in (10, 8, 6, 4, 2, 0):
        sign = -1.0 if (order // 2) % 2 else 1.0
        cosine = cosine * square + f32(sign / math.factorial(order))
    sine = sine * half
    return 2.0 * sine * cosine, 1.0 - 2.0 * sine * sine


def wrap(value, modulus):
    return value & (modulus - 1) if modulus & (modulus - 1) == 0 else lax.rem(value, modulus)


def log_sum(terms):
    top = functools.reduce(jnp.maximum, terms)
    total = functools.reduce(jnp.add, [jnp.exp2(term - top) for term in terms])
    return top + jnp.log(total) * f32(log2_e)


def chunk_lse(left, right):
    scores = lax.dot_general(
        left, right, (((1,), (1,)), ((), ())), preferred_element_type=f32
    )
    top = jnp.max(scores, 0, keepdims=True)
    total = jnp.sum(jnp.exp2(scores - top), 0, keepdims=True)
    return top + jnp.log(total) * f32(log2_e)


def place(values, static, left_ref):
    blocks = values.shape[0]
    high = values.astype(bf16).astype(f32)
    rest = values - high
    mid = rest.astype(bf16).astype(f32)
    low = rest - mid
    filler = [jnp.zeros((LANES // 2, LANES), f32), high, mid, low]
    spare = LANES // 2 - 3 * blocks
    if spare:
        filler.append(jnp.zeros((spare, LANES), f32))
    turned = jnp.concatenate(filler, 0).T
    lane = lax.broadcasted_iota(jnp.int32, (LANES, LANES), 1)
    for block in range(blocks):
        rows = pl.ds(block * LANES, LANES)
        kept = jnp.where(
            lane < LANES // 2,
            static[rows, LANES:].astype(f32),
            jnp.where(lax.rem(lane - LANES // 2, blocks) == block, turned, 0.0),
        )
        left_ref[rows, LANES:] = kept.astype(bf16)


def kernel(
    sizes, generator_ref, shift_ref, targets_ref, weights_ref, f_ref, g_ref,
    a_left, a_right, b_left, b_right, squares, pair, far_ref, near_ref,
    row_out, row_in, col_out, col_in, norm_out, norm_in,
    row_send, row_recv, col_send, col_recv, norm_send, norm_recv,
):
    src, tgt = sizes
    modulus = SRC_DEV * src
    my_src, my_tgt = lax.axis_index("src"), lax.axis_index("tgt")
    src_peers = [lax.rem(my_src + step, src) for step in range(1, src)]
    tgt_peers = [lax.rem(my_tgt + step, tgt) for step in range(1, tgt)]
    barrier = pltpu.get_barrier_semaphore()
    for peer in tgt_peers:
        pl.semaphore_signal(barrier, inc=1, device_id=(my_src, peer), device_id_type=MESH)
    for peer in src_peers:
        pl.semaphore_signal(barrier, inc=1, device_id=(peer, my_tgt), device_id_type=MESH)

    def row_copy(step, number):
        return pltpu.make_async_remote_copy(
            src_ref=row_out.at[step], dst_ref=row_in.at[step, number],
            send_sem=row_send.at[step, number], recv_sem=row_recv.at[step, number],
            device_id=(my_src, tgt_peers[number]), device_id_type=MESH,
        )

    def col_copy(step, number):
        return pltpu.make_async_remote_copy(
            src_ref=col_out.at[step], dst_ref=col_in.at[step, number],
            send_sem=col_send.at[step, number], recv_sem=col_recv.at[step, number],
            device_id=(src_peers[number], my_tgt), device_id_type=MESH,
        )

    def norm_copy(number):
        return pltpu.make_async_remote_copy(
            src_ref=norm_out, dst_ref=norm_in.at[number],
            send_sem=norm_send.at[number], recv_sem=norm_recv.at[number],
            device_id=(my_src, tgt_peers[number]), device_id_type=MESH,
        )

    blocks_i = SRC_DEV // LANES
    columns = targets_ref.shape[1]
    blocks_j = columns // LANES
    lane = lax.broadcasted_iota(jnp.int32, (LANES, LANES), 1)
    first = lane < LANES // 2

    pair[0:1, : LANES // 2] = generator_ref[...].astype(f32)
    pair[1:2, : LANES // 2] = shift_ref[...]
    both = pair[0:2, :]
    low_half = lax.broadcasted_iota(jnp.int32, (2, LANES), 1) < LANES // 2
    both = jnp.where(low_half, both, pltpu.roll(both, LANES // 2, 1))
    generator = both[0:1, :].astype(jnp.int32)
    shift = both[1:2, :]
    inner = lax.broadcasted_iota(jnp.int32, (LANES, LANES), 0)
    sin_in, cos_in = sine_cosine(
        wrap(inner * generator, modulus).astype(f32) / modulus
    )
    outer = lax.broadcasted_iota(jnp.int32, (blocks_i, LANES), 0) * LANES + my_src * SRC_DEV
    sin_out, cos_out = sine_cosine(
        wrap(outer * generator, modulus).astype(f32) / modulus + shift
    )
    for block in range(blocks_i):
        rows = pl.ds(block * LANES, LANES)
        points = (
            sin_out[block : block + 1, :] * cos_in + cos_out[block : block + 1, :] * sin_in
        )
        high = points.astype(bf16)
        a_left[rows, :LANES] = high
        a_right[rows, :LANES] = high
        a_right[rows, LANES:] = jnp.where(first, points - high.astype(f32), 1.0).astype(bf16)
        square = points * points
        square_high = square.astype(bf16).astype(f32)
        squares[rows, :] = jnp.where(first, square_high, square - square_high).astype(bf16)

    for block in range(blocks_j):
        rows = pl.ds(block * LANES, LANES)
        part = targets_ref[:, block * LANES : (block + 1) * LANES]
        far_ref[block : block + 1, :] = 0.5 * jnp.sum(part * part, 0, keepdims=True)
        part = part * f32(scale)
        high = part.astype(bf16).astype(f32)
        turned = jnp.concatenate([high, part - high], 0).T
        b_left[rows, :LANES] = turned.astype(bf16)
        b_right[rows, :LANES] = turned.astype(bf16)
        b_right[rows, LANES:] = jnp.where(first, turned, 1.0).astype(bf16)

    weights = weights_ref[...] * f32(log2_e)
    far = far_ref[...] * f32(scale)
    log_count = f32(math.log2(modulus))
    potential_g = -far
    for step in range(ITERS):
        place(weights + potential_g, b_right, b_left)
        for chunk in range(SRC_DEV // WIDE):
            part = chunk_lse(b_left[...], a_right[pl.ds(chunk * WIDE, WIDE), :])
            for piece in range(WIDE // LANES):
                at = chunk * (WIDE // LANES) + piece
                row_out[step, at : at + 1, :] = part[:, piece * LANES : (piece + 1) * LANES]
        if step == 0:
            peak = jnp.max(weights, keepdims=True)
            total = jnp.sum(jnp.exp2(weights - peak), keepdims=True)
            norm_out[...] = jnp.broadcast_to(
                peak + jnp.log(total) * f32(log2_e), (8, LANES)
            )
            pl.semaphore_wait(barrier, src - 1 + tgt - 1)
        for number in range(tgt - 1):
            row_copy(step, number).start()
        if step == 0:
            for number in range(tgt - 1):
                norm_copy(number).start()
            sums = lax.dot_general(
                jnp.ones((8, LANES), bf16), squares[...],
                (((1,), (1,)), ((), ())), preferred_element_type=f32,
            )
            for block in range(blocks_i):
                near_ref[block : block + 1, :] = (
                    0.5 * sums[0:1, block * LANES : (block + 1) * LANES]
                )
        for number in range(tgt - 1):
            row_copy(step, number).wait_recv()
        potential_f = -log_sum(
            [row_out[step]] + [row_in[step, number] for number in range(tgt - 1)]
        )
        place(potential_f, a_right, a_left)
        for chunk in range(columns // WIDE):
            part = chunk_lse(a_left[...], b_right[pl.ds(chunk * WIDE, WIDE), :])
            for piece in range(WIDE // LANES):
                at = chunk * (WIDE // LANES) + piece
                col_out[step, at : at + 1, :] = part[:, piece * LANES : (piece + 1) * LANES]
        for number in range(src - 1):
            col_copy(step, number).start()
        if step == 0:
            for number in range(tgt - 1):
                norm_copy(number).wait_recv()
            norm = log_sum(
                [norm_out[...]] + [norm_in[number] for number in range(tgt - 1)]
            )[0:1, :]
        if step == ITERS - 1:
            f_ref[...] = (potential_f + norm) * f32(1.0 / scale) + near_ref[...]
        for number in range(src - 1):
            col_copy(step, number).wait_recv()
        sums = log_sum([col_out[step]] + [col_in[step, number] for number in range(src - 1)])
        potential_g = log_count - sums - norm
    g_ref[...] = potential_g * f32(1.0 / scale) + far_ref[...]
    for step in range(ITERS):
        for number in range(tgt - 1):
            row_copy(step, number).wait_send()
        for number in range(src - 1):
            col_copy(step, number).wait_send()
    for number in range(tgt - 1):
        norm_copy(number).wait_send()


def local(sizes, generator, shift, targets, log_weights):
    src, tgt = sizes
    columns = targets.shape[1]
    blocks_i, blocks_j = SRC_DEV // LANES, columns // LANES
    vmem = pl.BlockSpec(memory_space=pltpu.VMEM)
    dma = pltpu.SemaphoreType.DMA
    potential_f, potential_g = pl.pallas_call(
        functools.partial(kernel, sizes),
        out_shape=(
            jax.ShapeDtypeStruct((blocks_i, LANES), f32),
            jax.ShapeDtypeStruct((blocks_j, LANES), f32),
        ),
        in_specs=[vmem] * 4,
        out_specs=(vmem, vmem),
        scratch_shapes=[
            pltpu.VMEM((SRC_DEV, 2 * LANES), bf16),
            pltpu.VMEM((SRC_DEV, 2 * LANES), bf16),
            pltpu.VMEM((columns, 2 * LANES), bf16),
            pltpu.VMEM((columns, 2 * LANES), bf16),
            pltpu.VMEM((SRC_DEV, LANES), bf16),
            pltpu.VMEM((8, LANES), f32),
            pltpu.VMEM((blocks_j, LANES), f32),
            pltpu.VMEM((blocks_i, LANES), f32),
            pltpu.VMEM((ITERS, blocks_i, LANES), f32),
            pltpu.VMEM((ITERS, tgt - 1, blocks_i, LANES), f32),
            pltpu.VMEM((ITERS, blocks_j, LANES), f32),
            pltpu.VMEM((ITERS, src - 1, blocks_j, LANES), f32),
            pltpu.VMEM((8, LANES), f32),
            pltpu.VMEM((tgt - 1, 8, LANES), f32),
            dma((ITERS, tgt - 1)),
            dma((ITERS, tgt - 1)),
            dma((ITERS, src - 1)),
            dma((ITERS, src - 1)),
            dma((tgt - 1,)),
            dma((tgt - 1,)),
        ],
        compiler_params=pltpu.CompilerParams(
            collective_id=0, has_side_effects=True, vmem_limit_bytes=40 * 2**20
        ),
    )(
        generator.reshape(1, -1),
        shift.reshape(1, -1),
        targets,
        log_weights.reshape(blocks_j, LANES),
    )
    return potential_f.reshape(-1), potential_g.reshape(-1)


def solution(mesh):
    sizes = (mesh.shape["src"], mesh.shape["tgt"])
    in_specs = (P(), P(), P(None, "tgt"), P("tgt"))
    out_specs = (P("src"), P("tgt"))
    return jax.shard_map(
        functools.partial(local, sizes), mesh=mesh,
        in_specs=in_specs, out_specs=out_specs, check_vma=False,
    )
```

time: 237 us -> 30.3 us (0.13)
  blocking collectives: 83 us -> 0 us
  matrix products: 59.7 us -> 0 us
  other arithmetic: 33.2 us -> 0 us
  Pallas kernels: 0 us -> 26.6 us
  waiting for transfers between devices: 17.2 us -> 0 us
  starting transfers between devices: 13.3 us -> 0 us
  local copies, waits for them, and re-layouts: 14.2 us -> 2.81 us
  loops' own time: 11.3 us -> 0 us
  between operations: 4.18 us -> 0.67 us
    dot_general x16 -> x0, matrix products: 59.7 us -> none  [cost_block(): lax.dot_general(points, targets, (((0,), (0,)), ((), ())), precision=high...]
    pmax x3 -> x0, blocking collectives: 38.1 us -> none  [the longest x2 22.3 us: column_reduce(): top = lax.pmax(peak, 'src')]
    reduce_sum x36 -> x0, other arithmetic: 30.2 us -> none  [the longest x16 20.4 us: cost_block(): near = 0.5 * jnp.sum(points * points, 0)]
    psum x3 -> x0, blocking collectives: 29 us -> none  [the longest x2 16.7 us: column_reduce(): summed = lax.psum(total * jnp.exp(peak - top), 'src')]
    pallas_call x0 -> x1, Pallas kernels: none -> 26.6 us  [local(): pl.pallas_call(functools.partial(kernel, sizes), out_shape=(jax.ShapeDtyp...]
    all_to_all x4 -> x0, waiting for transfers between devices: 17.2 us -> none  [the longest x2 9.18 us: row_reduce(): lax.all_to_all(total[None, :], 'tgt', split_axis=1, concat_axis=0, tiled=...]
    all_gather x2 -> x0, blocking collectives: 15.9 us -> none  [row_reduce(): return lax.all_gather(share, 'tgt', axis=0, tiled=True)]
    all_to_all x4 -> x0, starting transfers between devices: 13.3 us -> none  [the longest x2 6.67 us: row_reduce(): lax.all_to_all(peak[None, :], 'tgt', split_axis=1, concat_axis=0, tiled=T...]
  transfers between devices with their start and end apart: 4 -> 0, of which waited for: 4 -> 0; matrix products, arithmetic and copies ran while one was open for 0% -> 0% of each run, Pallas kernels for 0% -> 0%
where the time goes in v1:
time: 30.3 us; the launch traced here: 30.1 us
  Pallas kernels  26.6 us (88%)
  local copies, waits for them, and re-layouts  2.81 us (9%)
  between operations  0.67 us (2%)
    pallas_call x1, Pallas kernels, local(): pl.pallas_call(functools.partial(kernel, sizes), out_shape=(jax.ShapeDtyp...  26.6 us
    unnamed x10, local copies, waits for them, and re-layouts  2.81 us

profile of v1, /device:TPU:0, one launch (start us, length us, event | category | flops | bytes accessed | tf_op | source)
XLA Modules:
  0.0 30.1 jit_solution(9366402335079185467)
XLA Ops:
  0.6 0.0 copy-start.1
  0.6 0.0 copy-start.2
  0.7 0.0 copy-start.3
  0.7 0.7 %copy-done.1 = f32[1024]{0:T(1024)S(1)} copy-done((f32[1024]{0:T(1024)S(1)}, f32[1024]{0:T(1024)}, u32[]{:S(2)}) %copy-start.1) | copy-done | bytes 4120
  1.3 0.0 copy-done.2
  1.3 0.0 copy-done.3
  1.3 0.0 copy-start
  1.3 0.9 %copy-done = f32[64,1024]{1,0:T(8,128)S(1)} copy-done((f32[64,1024]{1,0:T(8,128)S(1)}, f32[64,1024]{1,0:T(8,128)}, u32[]{:S(2)}) %copy-start) | copy-done | bytes 262168
  2.3 26.6 %shard_map.59 = (f32[16,128]{1,0:T(8,128)S(1)}, f32[8,128]{1,0:T(8,128)S(1)}) custom-call(s32[1,64]{1,0:T(1,128)S(1)} %bitcast.8, f32[1,64]{1,0:T(1,128)S(1)} %bitcast.9, f32[64,1024]{1,0:T(8,128)S(1)} %copy-done, f32[8,128]{1,0:T(8,128)S(1)} %bitcast.6), custom_call_target="tpu_custom_call" | custom-call | tf_op jit(solution)/shard_map/pallas_call | solution.py:235
  28.9 0.6 %copy.8 = f32[2048]{0:T(1024)} copy(f32[2048]{0:T(1024)S(1)} %bitcast.5) | data formatting | bytes 16384
  29.5 0.6 %copy.9 = f32[1024]{0:T(1024)} copy(f32[1024]{0:T(1024)S(1)} %bitcast.7) | data formatting | bytes 8192
Async XLA Ops:
  0.6 0.7 %copy-start.1 = (f32[1024]{0:T(1024)S(1)}, f32[1024]{0:T(1024)}, u32[]{:S(2)}) copy-start(f32[1024]{0:T(1024)} %param.7) | copy-start | bytes 12292
  0.6 0.7 %copy-start.2 = (s32[64]{0:T(128)S(1)}, s32[64]{0:T(128)}, u32[]{:S(2)}) copy-start(s32[64]{0:T(128)} %param.4) | copy-start | bytes 772
  0.7 0.7 %copy-start.3 = (f32[64]{0:T(128)S(1)}, f32[64]{0:T(128)}, u32[]{:S(2)}) copy-start(f32[64]{0:T(128)} %param.5) | copy-start | bytes 772
  1.3 1.0 %copy-start = (f32[64,1024]{1,0:T(8,128)S(1)}, f32[64,1024]{1,0:T(8,128)}, u32[]{:S(2)}) copy-start(f32[64,1024]{1,0:T(8,128)} %targets_ref.1) | copy-start | bytes 786436

commit v2 on v1

--- a/solution.py
+++ b/solution.py
@@ -12,6 +12,7 @@
 ITERS = 2
 LANES = 128
 WIDE = 256
+GROUP = 8
 
 blur_level = 0.1
 log2_e = math.log2(math.e)
@@ -46,13 +47,29 @@
     return top + jnp.log(total) * f32(log2_e)
 
 
-def chunk_lse(left, right):
-    scores = lax.dot_general(
-        left, right, (((1,), (1,)), ((), ())), preferred_element_type=f32
-    )
-    top = jnp.max(scores, 0, keepdims=True)
-    total = jnp.sum(jnp.exp2(scores - top), 0, keepdims=True)
-    return top + jnp.log(total) * f32(log2_e)
+def fold(combine, scores):
+    parts = scores.reshape(-1, 8 * GROUP, scores.shape[1])
+    return combine(combine(parts, 0), 0, keepdims=True)
+
+
+def sweep(left_ref, right_ref, count, tops, totals):
+    def product(chunk):
+        return lax.dot_general(
+            left_ref[...], right_ref[pl.ds(chunk * WIDE, WIDE), :],
+            (((1,), (1,)), ((), ())), preferred_element_type=f32,
+        )
+
+    scores = product(0)
+    for chunk in range(count):
+        later = product(chunk + 1) if chunk + 1 < count else None
+        top = fold(jnp.max, scores)
+        total = fold(jnp.sum, jnp.exp2(scores - top))
+        for piece in range(WIDE // LANES):
+            at = chunk * (WIDE // LANES) + piece
+            cut = slice(piece * LANES, (piece + 1) * LANES)
+            tops[at : at + 1, :] = top[:, cut]
+            totals[at : at + 1, :] = total[:, cut]
+        scores = later
 
 
 def place(values, static, left_ref):
@@ -78,16 +95,27 @@
 
 
 def kernel(
-    sizes, generator_ref, shift_ref, targets_ref, weights_ref, f_ref, g_ref,
+    sizes, generator_hbm, shift_hbm, targets_hbm, weights_hbm, f_ref, g_ref,
+    generator_ref, shift_ref, targets_ref, weights_ref,
     a_left, a_right, b_left, b_right, squares, pair, far_ref, near_ref,
+    row_tops, row_totals, col_tops, col_totals,
     row_out, row_in, col_out, col_in, norm_out, norm_in,
-    row_send, row_recv, col_send, col_recv, norm_send, norm_recv,
+    row_send, row_recv, col_send, col_recv, norm_send, norm_recv, load,
 ):
     src, tgt = sizes
     modulus = SRC_DEV * src
     my_src, my_tgt = lax.axis_index("src"), lax.axis_index("tgt")
     src_peers = [lax.rem(my_src + step, src) for step in range(1, src)]
     tgt_peers = [lax.rem(my_tgt + step, tgt) for step in range(1, tgt)]
+    loads = [
+        pltpu.make_async_copy(source, place_in, load.at[number])
+        for number, (source, place_in) in enumerate((
+            (generator_hbm, generator_ref), (shift_hbm, shift_ref),
+            (targets_hbm, targets_ref), (weights_hbm, weights_ref),
+        ))
+    ]
+    for copy in loads:
+        copy.start()
     barrier = pltpu.get_barrier_semaphore()
     for peer in tgt_peers:
         pl.semaphore_signal(barrier, inc=1, device_id=(my_src, peer), device_id_type=MESH)
@@ -121,6 +149,8 @@
     lane = lax.broadcasted_iota(jnp.int32, (LANES, LANES), 1)
     first = lane < LANES // 2
 
+    loads[0].wait()
+    loads[1].wait()
     pair[0:1, : LANES // 2] = generator_ref[...].astype(f32)
     pair[1:2, : LANES // 2] = shift_ref[...]
     both = pair[0:2, :]
@@ -149,6 +179,8 @@
         square_high = square.astype(bf16).astype(f32)
         squares[rows, :] = jnp.where(first, square_high, square - square_high).astype(bf16)
 
+    loads[2].wait()
+    loads[3].wait()
     for block in range(blocks_j):
         rows = pl.ds(block * LANES, LANES)
         part = targets_ref[:, block * LANES : (block + 1) * LANES]
@@ -166,11 +198,8 @@
     potential_g = -far
     for step in range(ITERS):
         place(weights + potential_g, b_right, b_left)
-        for chunk in range(SRC_DEV // WIDE):
-            part = chunk_lse(b_left[...], a_right[pl.ds(chunk * WIDE, WIDE), :])
-            for piece in range(WIDE // LANES):
-                at = chunk * (WIDE // LANES) + piece
-                row_out[step, at : at + 1, :] = part[:, piece * LANES : (piece + 1) * LANES]
+        sweep(b_left, a_right, SRC_DEV // WIDE, row_tops, row_totals)
+        row_out[step] = row_tops[...] + jnp.log(row_totals[...]) * f32(log2_e)
         if step == 0:
             peak = jnp.max(weights, keepdims=True)
             total = jnp.sum(jnp.exp2(weights - peak), keepdims=True)
@@ -197,11 +226,8 @@
             [row_out[step]] + [row_in[step, number] for number in range(tgt - 1)]
         )
         place(potential_f, a_right, a_left)
-        for chunk in range(columns // WIDE):
-            part = chunk_lse(a_left[...], b_right[pl.ds(chunk * WIDE, WIDE), :])
-            for piece in range(WIDE // LANES):
-                at = chunk * (WIDE // LANES) + piece
-                col_out[step, at : at + 1, :] = part[:, piece * LANES : (piece + 1) * LANES]
+        sweep(a_left, b_right, columns // WIDE, col_tops, col_totals)
+        col_out[step] = col_tops[...] + jnp.log(col_totals[...]) * f32(log2_e)
         for number in range(src - 1):
             col_copy(step, number).start()
         if step == 0:
@@ -238,9 +264,13 @@
             jax.ShapeDtypeStruct((blocks_i, LANES), f32),
             jax.ShapeDtypeStruct((blocks_j, LANES), f32),
         ),
-        in_specs=[vmem] * 4,
+        in_specs=[pl.BlockSpec(memory_space=pltpu.HBM)] * 4,
         out_specs=(vmem, vmem),
         scratch_shapes=[
+            pltpu.VMEM((1, generator.shape[0]), jnp.int32),
+            pltpu.VMEM((1, shift.shape[0]), f32),
+            pltpu.VMEM(targets.shape, f32),
+            pltpu.VMEM((blocks_j, LANES), f32),
             pltpu.VMEM((SRC_DEV, 2 * LANES), bf16),
             pltpu.VMEM((SRC_DEV, 2 * LANES), bf16),
             pltpu.VMEM((columns, 2 * LANES), bf16),
@@ -249,6 +279,10 @@
             pltpu.VMEM((8, LANES), f32),
             pltpu.VMEM((blocks_j, LANES), f32),
             pltpu.VMEM((blocks_i, LANES), f32),
+            pltpu.VMEM((blocks_i, LANES), f32),
+            pltpu.VMEM((blocks_i, LANES), f32),
+            pltpu.VMEM((blocks_j, LANES), f32),
+            pltpu.VMEM((blocks_j, LANES), f32),
             pltpu.VMEM((ITERS, blocks_i, LANES), f32),
             pltpu.VMEM((ITERS, tgt - 1, blocks_i, LANES), f32),
             pltpu.VMEM((ITERS, blocks_j, LANES), f32),
@@ -261,9 +295,10 @@
             dma((ITERS, src - 1)),
             dma((tgt - 1,)),
             dma((tgt - 1,)),
+            dma((4,)),
         ],
         compiler_params=pltpu.CompilerParams(
-            collective_id=0, has_side_effects=True, vmem_limit_bytes=40 * 2**20
+            collective_id=0, has_side_effects=True, vmem_limit_bytes=64 * 2**20 - 2**17
         ),
     )(
         generator.reshape(1, -1),

time: 30.3 us -> 30.2 us (level)
  local copies, waits for them, and re-layouts: 2.81 us -> 1.89 us
  Pallas kernels: 26.6 us -> 27.4 us
    unnamed x10 -> x4, local copies, waits for them, and re-layouts: 2.81 us -> 1.89 us
    pallas_call x1, Pallas kernels: 26.6 us -> 27.4 us  [local(): pl.pallas_call(functools.partial(kernel, sizes), out_shape=(jax.ShapeDtyp...]
where the time goes in v2:
time: 30.2 us; the launch traced here: 30 us
  Pallas kernels  27.4 us (91%)
  local copies, waits for them, and re-layouts  1.89 us (6%)
  between operations  0.65 us (2%)
    pallas_call x1, Pallas kernels, local(): pl.pallas_call(functools.partial(kernel, sizes), out_shape=(jax.ShapeDtyp...  27.4 us
    unnamed x4, local copies, waits for them, and re-layouts  1.89 us

profile of v2, /device:TPU:0, one launch (start us, length us, event | category | flops | bytes accessed | tf_op | source)
XLA Modules:
  0.0 30.0 jit_solution(14074080463560699718)
XLA Ops:
  0.6 27.4 %shard_map.59 = (f32[16,128]{1,0:T(8,128)}, f32[8,128]{1,0:T(8,128)}) custom-call(s32[1,64]{1,0:T(1,128)} %bitcast.8, f32[1,64]{1,0:T(1,128)} %bitcast.9, f32[64,1024]{1,0:T(8,128)} %targets_hbm.1, f32[8,128]{1,0:T(8,128)} %bitcast.6), custom_call_target="tpu_custom_call" | custom-call | tf_op jit(solution)/shard_map/pallas_call | solution.py:261
  28.1 0.0 copy-start
  28.1 1.3 %copy.8 = f32[2048]{0:T(1024)} copy(f32[2048]{0:T(1024)} %bitcast.5) | data formatting | bytes 16384
  29.4 0.0 copy-done
  29.4 0.6 %copy.9 = f32[1024]{0:T(1024)} copy(f32[1024]{0:T(1024)S(1)} %bitcast.7) | data formatting | bytes 8192
Async XLA Ops:
  28.1 1.3 %copy-start = (f32[8,128]{1,0:T(8,128)S(1)}, f32[8,128]{1,0:T(8,128)}, u32[]{:S(2)}) copy-start(f32[8,128]{1,0:T(8,128)} %get-tuple-element.5) | copy-start | bytes 12292

commit v3 on v2

--- a/solution.py
+++ b/solution.py
@@ -12,7 +12,9 @@
 ITERS = 2
 LANES = 128
 WIDE = 256
-GROUP = 8
+TILE = 64
+LIMIT = 40 * 2**20
+PRODUCT = 1024
 
 blur_level = 0.1
 log2_e = math.log2(math.e)
@@ -47,29 +49,43 @@
     return top + jnp.log(total) * f32(log2_e)
 
 
-def fold(combine, scores):
-    parts = scores.reshape(-1, 8 * GROUP, scores.shape[1])
-    return combine(combine(parts, 0), 0, keepdims=True)
-
-
-def sweep(left_ref, right_ref, count, tops, totals):
+def fold(combine, scores, rows):
+    running = None
+    for start in range(0, rows, TILE):
+        running = combine(running, scores[pl.ds(start, TILE), :])
+    return running
+
+
+def sweep(left_ref, right_ref, buffers, tops, totals):
+    rows, count = left_ref.shape[0], right_ref.shape[1] // WIDE
+
     def product(chunk):
-        return lax.dot_general(
-            left_ref[...], right_ref[pl.ds(chunk * WIDE, WIDE), :],
-            (((1,), (1,)), ((), ())), preferred_element_type=f32,
-        )
-
-    scores = product(0)
+        right = right_ref[:, pl.ds(chunk * WIDE, WIDE)]
+        for start in range(0, rows, PRODUCT):
+            part = pl.ds(start, PRODUCT)
+            buffers[chunk % 2][part, :] = jnp.dot(
+                left_ref[part, :], right, preferred_element_type=f32
+            )
+
+    product(0)
     for chunk in range(count):
-        later = product(chunk + 1) if chunk + 1 < count else None
-        top = fold(jnp.max, scores)
-        total = fold(jnp.sum, jnp.exp2(scores - top))
+        if chunk + 1 < count:
+            product(chunk + 1)
+        scores = buffers[chunk % 2]
+        top = fold(lambda a, b: b if a is None else jnp.maximum(a, b), scores, rows)
+        top = jnp.max(top, 0, keepdims=True)
+        shift = jnp.broadcast_to(top, (TILE, WIDE))
+
+        def add(total, part):
+            part = jnp.exp2(part - shift)
+            return part if total is None else total + part
+
+        total = jnp.sum(fold(add, scores, rows), 0, keepdims=True)
         for piece in range(WIDE // LANES):
             at = chunk * (WIDE // LANES) + piece
             cut = slice(piece * LANES, (piece + 1) * LANES)
             tops[at : at + 1, :] = top[:, cut]
             totals[at : at + 1, :] = total[:, cut]
-        scores = later
 
 
 def place(values, static, left_ref):
@@ -84,20 +100,17 @@
         filler.append(jnp.zeros((spare, LANES), f32))
     turned = jnp.concatenate(filler, 0).T
     lane = lax.broadcasted_iota(jnp.int32, (LANES, LANES), 1)
+    owner = jnp.where(lane < LANES // 2, -1, wrap(lane, blocks))
     for block in range(blocks):
         rows = pl.ds(block * LANES, LANES)
-        kept = jnp.where(
-            lane < LANES // 2,
-            static[rows, LANES:].astype(f32),
-            jnp.where(lax.rem(lane - LANES // 2, blocks) == block, turned, 0.0),
-        )
-        left_ref[rows, LANES:] = kept.astype(bf16)
+        added = jnp.where(owner == block, turned, 0.0).astype(bf16)
+        left_ref[rows, LANES:] = static[rows, :] + added
 
 
 def kernel(
-    sizes, generator_hbm, shift_hbm, targets_hbm, weights_hbm, f_ref, g_ref,
+    sizes, generator_hbm, shift_hbm, targets_hbm, weights_hbm, out_ref,
     generator_ref, shift_ref, targets_ref, weights_ref,
-    a_left, a_right, b_left, b_right, squares, pair, far_ref, near_ref,
+    a_left, a_right, a_static, b_left, b_right, b_static, buffer_0, buffer_1, pair, far_ref, near_ref,
     row_tops, row_totals, col_tops, col_totals,
     row_out, row_in, col_out, col_in, norm_out, norm_in,
     row_send, row_recv, col_send, col_recv, norm_send, norm_recv, load,
@@ -166,6 +179,7 @@
     sin_out, cos_out = sine_cosine(
         wrap(outer * generator, modulus).astype(f32) / modulus + shift
     )
+    half = LANES // 2
     for block in range(blocks_i):
         rows = pl.ds(block * LANES, LANES)
         points = (
@@ -173,11 +187,23 @@
         )
         high = points.astype(bf16)
         a_left[rows, :LANES] = high
-        a_right[rows, :LANES] = high
-        a_right[rows, LANES:] = jnp.where(first, points - high.astype(f32), 1.0).astype(bf16)
-        square = points * points
-        square_high = square.astype(bf16).astype(f32)
-        squares[rows, :] = jnp.where(first, square_high, square - square_high).astype(bf16)
+        a_static[rows, :] = jnp.where(first, points - high.astype(f32), 0.0).astype(bf16)
+    sin_in, cos_in = sin_in.T[:half, :], cos_in.T[:half, :]
+    outside = jnp.concatenate(
+        [sin_out, cos_out, jnp.zeros((LANES - 2 * blocks_i, LANES), f32)], 0
+    ).T[:half, :]
+    for block in range(blocks_i):
+        cut = pl.ds(block * LANES, LANES)
+        points = (
+            outside[:, block : block + 1] * cos_in
+            + outside[:, blocks_i + block : blocks_i + block + 1] * sin_in
+        )
+        near_ref[block : block + 1, :] = 0.5 * jnp.sum(points * points, 0, keepdims=True)
+        high = points.astype(bf16)
+        a_right[:half, cut] = high
+        a_right[half : 2 * half, cut] = high
+        a_right[2 * half : 3 * half, cut] = (points - high.astype(f32)).astype(bf16)
+    a_right[3 * half :, :] = jnp.ones((half, SRC_DEV), bf16)
 
     loads[2].wait()
     loads[3].wait()
@@ -186,19 +212,24 @@
         part = targets_ref[:, block * LANES : (block + 1) * LANES]
         far_ref[block : block + 1, :] = 0.5 * jnp.sum(part * part, 0, keepdims=True)
         part = part * f32(scale)
-        high = part.astype(bf16).astype(f32)
-        turned = jnp.concatenate([high, part - high], 0).T
+        high = part.astype(bf16)
+        low = part - high.astype(f32)
+        turned = jnp.concatenate([high.astype(f32), low], 0).T
         b_left[rows, :LANES] = turned.astype(bf16)
-        b_right[rows, :LANES] = turned.astype(bf16)
-        b_right[rows, LANES:] = jnp.where(first, turned, 1.0).astype(bf16)
+        b_static[rows, :] = jnp.where(first, turned, 0.0).astype(bf16)
+        b_right[:half, rows] = high
+        b_right[half : 2 * half, rows] = low.astype(bf16)
+        b_right[2 * half : 3 * half, rows] = high
+    b_right[3 * half :, :] = jnp.ones((half, columns), bf16)
 
     weights = weights_ref[...] * f32(log2_e)
     far = far_ref[...] * f32(scale)
     log_count = f32(math.log2(modulus))
     potential_g = -far
+    buffers = (buffer_0, buffer_1)
     for step in range(ITERS):
-        place(weights + potential_g, b_right, b_left)
-        sweep(b_left, a_right, SRC_DEV // WIDE, row_tops, row_totals)
+        place(weights + potential_g, b_static, b_left)
+        sweep(b_left, a_right, buffers, row_tops, row_totals)
         row_out[step] = row_tops[...] + jnp.log(row_totals[...]) * f32(log2_e)
         if step == 0:
             peak = jnp.max(weights, keepdims=True)
@@ -212,21 +243,13 @@
         if step == 0:
             for number in range(tgt - 1):
                 norm_copy(number).start()
-            sums = lax.dot_general(
-                jnp.ones((8, LANES), bf16), squares[...],
-                (((1,), (1,)), ((), ())), preferred_element_type=f32,
-            )
-            for block in range(blocks_i):
-                near_ref[block : block + 1, :] = (
-                    0.5 * sums[0:1, block * LANES : (block + 1) * LANES]
-                )
         for number in range(tgt - 1):
             row_copy(step, number).wait_recv()
         potential_f = -log_sum(
             [row_out[step]] + [row_in[step, number] for number in range(tgt - 1)]
         )
-        place(potential_f, a_right, a_left)
-        sweep(a_left, b_right, columns // WIDE, col_tops, col_totals)
+        place(potential_f, a_static, a_left)
+        sweep(a_left, b_right, buffers, col_tops, col_totals)
         col_out[step] = col_tops[...] + jnp.log(col_totals[...]) * f32(log2_e)
         for number in range(src - 1):
             col_copy(step, number).start()
@@ -237,12 +260,12 @@
                 [norm_out[...]] + [norm_in[number] for number in range(tgt - 1)]
             )[0:1, :]
         if step == ITERS - 1:
-            f_ref[...] = (potential_f + norm) * f32(1.0 / scale) + near_ref[...]
+            out_ref[:blocks_i, :] = (potential_f + norm) * f32(1.0 / scale) + near_ref[...]
         for number in range(src - 1):
             col_copy(step, number).wait_recv()
         sums = log_sum([col_out[step]] + [col_in[step, number] for number in range(src - 1)])
         potential_g = log_count - sums - norm
-    g_ref[...] = potential_g * f32(1.0 / scale) + far_ref[...]
+    out_ref[blocks_i:, :] = potential_g * f32(1.0 / scale) + far_ref[...]
     for step in range(ITERS):
         for number in range(tgt - 1):
             row_copy(step, number).wait_send()
@@ -258,24 +281,24 @@
     blocks_i, blocks_j = SRC_DEV // LANES, columns // LANES
     vmem = pl.BlockSpec(memory_space=pltpu.VMEM)
     dma = pltpu.SemaphoreType.DMA
-    potential_f, potential_g = pl.pallas_call(
+    both = pl.pallas_call(
         functools.partial(kernel, sizes),
-        out_shape=(
-            jax.ShapeDtypeStruct((blocks_i, LANES), f32),
-            jax.ShapeDtypeStruct((blocks_j, LANES), f32),
-        ),
+        out_shape=jax.ShapeDtypeStruct((blocks_i + blocks_j, LANES), f32),
         in_specs=[pl.BlockSpec(memory_space=pltpu.HBM)] * 4,
-        out_specs=(vmem, vmem),
+        out_specs=vmem,
         scratch_shapes=[
             pltpu.VMEM((1, generator.shape[0]), jnp.int32),
             pltpu.VMEM((1, shift.shape[0]), f32),
             pltpu.VMEM(targets.shape, f32),
             pltpu.VMEM((blocks_j, LANES), f32),
             pltpu.VMEM((SRC_DEV, 2 * LANES), bf16),
-            pltpu.VMEM((SRC_DEV, 2 * LANES), bf16),
+            pltpu.VMEM((2 * LANES, SRC_DEV), bf16),
+            pltpu.VMEM((SRC_DEV, LANES), bf16),
             pltpu.VMEM((columns, 2 * LANES), bf16),
-            pltpu.VMEM((columns, 2 * LANES), bf16),
-            pltpu.VMEM((SRC_DEV, LANES), bf16),
+            pltpu.VMEM((2 * LANES, columns), bf16),
+            pltpu.VMEM((columns, LANES), bf16),
+            pltpu.VMEM((max(SRC_DEV, columns), WIDE), f32),
+            pltpu.VMEM((max(SRC_DEV, columns), WIDE), f32),
             pltpu.VMEM((8, LANES), f32),
             pltpu.VMEM((blocks_j, LANES), f32),
             pltpu.VMEM((blocks_i, LANES), f32),
@@ -298,7 +321,7 @@
             dma((4,)),
         ],
         compiler_params=pltpu.CompilerParams(
-            collective_id=0, has_side_effects=True, vmem_limit_bytes=64 * 2**20 - 2**17
+            collective_id=0, has_side_effects=True, vmem_limit_bytes=LIMIT
         ),
     )(
         generator.reshape(1, -1),
@@ -306,7 +329,7 @@
         targets,
         log_weights.reshape(blocks_j, LANES),
     )
-    return potential_f.reshape(-1), potential_g.reshape(-1)
+    return both[:blocks_i].reshape(-1), both[blocks_i:].reshape(-1)
 
 
 def solution(mesh):

time: 30.2 us -> 30 us (level)
  Pallas kernels: 27.4 us -> 26.3 us
  local copies, waits for them, and re-layouts: 1.89 us -> 2.81 us
    reshape x0 -> x2, local copies, waits for them, and re-layouts: none -> 1.19 us  [local(): return (both[:blocks_i].reshape(-1), both[blocks_i:].reshape(-1))]
    pallas_call x1, Pallas kernels: 27.4 us -> 26.3 us  [local(): pl.pallas_call(functools.partial(kernel, sizes), out_shape=jax.ShapeDtype...]
    unnamed x4 -> x8, local copies, waits for them, and re-layouts: 1.89 us -> 1.62 us
where the time goes in v3:
time: 30 us; the launch traced here: 29.8 us
  Pallas kernels  26.3 us (88%)
  local copies, waits for them, and re-layouts  2.81 us (9%)
  between operations  0.67 us (2%)
    pallas_call x1, Pallas kernels, local(): pl.pallas_call(functools.partial(kernel, sizes), out_shape=jax.ShapeDtype...  26.3 us
    unnamed x8, local copies, waits for them, and re-layouts  1.62 us
    reshape x2, local copies, waits for them, and re-layouts, local(): return (both[:blocks_i].reshape(-1), both[blocks_i:].reshape(-1))  1.19 us

profile of v3, /device:TPU:0, one launch (start us, length us, event | category | flops | bytes accessed | tf_op | source)
XLA Modules:
  0.0 29.8 jit_solution(10505100800010684528)
XLA Ops:
  0.6 0.0 copy-start.1
  0.6 0.0 copy-start.2
  0.7 0.0 copy-start.3
  0.7 0.7 %copy-done.1 = f32[1024]{0:T(1024)S(1)} copy-done((f32[1024]{0:T(1024)S(1)}, f32[1024]{0:T(1024)}, u32[]{:S(2)}) %copy-start.1) | copy-done | bytes 4120
  1.3 0.0 copy-done.2
  1.3 0.0 copy-done.3
  1.3 0.0 copy-start
  1.3 0.9 %copy-done = f32[64,1024]{1,0:T(8,128)S(1)} copy-done((f32[64,1024]{1,0:T(8,128)S(1)}, f32[64,1024]{1,0:T(8,128)}, u32[]{:S(2)}) %copy-start) | copy-done | bytes 262168
  2.3 26.3 %shard_map.59 = f32[24,128]{1,0:T(8,128)S(1)} custom-call(s32[1,64]{1,0:T(1,128)S(1)} %bitcast.8, f32[1,64]{1,0:T(1,128)S(1)} %bitcast.9, f32[64,1024]{1,0:T(8,128)S(1)} %copy-done, f32[8,128]{1,0:T(8,128)S(1)} %bitcast.7), custom_call_target="tpu_custom_call" | custom-call | tf_op jit(solution)/shard_map/pallas_call | solution.py:284
  28.6 0.6 %slice_bitcast_fusion.1 = f32[1024]{0:T(1024)} fusion(f32[24,128]{1,0:T(8,128)S(1)} %shard_map.59), kind=kLoop, calls=%fused_computation.1 | loop fusion | bytes 8192 | tf_op jit(solution)/shard_map/reshape | solution.py:332
  29.2 0.6 %slice_bitcast_fusion = f32[2048]{0:T(1024)} fusion(f32[24,128]{1,0:T(8,128)S(1)} %shard_map.59), kind=kLoop, calls=%fused_computation | loop fusion | bytes 16384 | tf_op jit(solution)/shard_map/reshape | solution.py:332
Async XLA Ops:
  0.6 0.7 %copy-start.1 = (f32[1024]{0:T(1024)S(1)}, f32[1024]{0:T(1024)}, u32[]{:S(2)}) copy-start(f32[1024]{0:T(1024)} %param.7) | copy-start | bytes 12292
  0.6 0.7 %copy-start.2 = (s32[64]{0:T(128)S(1)}, s32[64]{0:T(128)}, u32[]{:S(2)}) copy-start(s32[64]{0:T(128)} %param.4) | copy-start | bytes 772
  0.7 0.7 %copy-start.3 = (f32[64]{0:T(128)S(1)}, f32[64]{0:T(128)}, u32[]{:S(2)}) copy-start(f32[64]{0:T(128)} %param.5) | copy-start | bytes 772
  1.3 1.0 %copy-start = (f32[64,1024]{1,0:T(8,128)S(1)}, f32[64,1024]{1,0:T(8,128)}, u32[]{:S(2)}) copy-start(f32[64,1024]{1,0:T(8,128)} %targets_hbm.1) | copy-start | bytes 786436

commit v4 on v3

--- a/solution.py
+++ b/solution.py
@@ -14,7 +14,7 @@
 WIDE = 256
 TILE = 64
 LIMIT = 40 * 2**20
-PRODUCT = 1024
+HALVES = 2
 
 blur_level = 0.1
 log2_e = math.log2(math.e)
@@ -56,23 +56,22 @@
     return running
 
 
-def sweep(left_ref, right_ref, buffers, tops, totals):
-    rows, count = left_ref.shape[0], right_ref.shape[1] // WIDE
+def sweep(left_ref, right_ref, buffers, rows, tops, totals, after=None):
+    first, size = rows
+    count = right_ref.shape[1] // WIDE
 
     def product(chunk):
         right = right_ref[:, pl.ds(chunk * WIDE, WIDE)]
-        for start in range(0, rows, PRODUCT):
-            part = pl.ds(start, PRODUCT)
-            buffers[chunk % 2][part, :] = jnp.dot(
-                left_ref[part, :], right, preferred_element_type=f32
-            )
+        buffers[chunk % 2][pl.ds(0, size), :] = jnp.dot(
+            left_ref[pl.ds(first, size), :], right, preferred_element_type=f32
+        )
 
     product(0)
     for chunk in range(count):
         if chunk + 1 < count:
             product(chunk + 1)
         scores = buffers[chunk % 2]
-        top = fold(lambda a, b: b if a is None else jnp.maximum(a, b), scores, rows)
+        top = fold(lambda a, b: b if a is None else jnp.maximum(a, b), scores, size)
         top = jnp.max(top, 0, keepdims=True)
         shift = jnp.broadcast_to(top, (TILE, WIDE))
 
@@ -80,15 +79,17 @@
             part = jnp.exp2(part - shift)
             return part if total is None else total + part
 
-        total = jnp.sum(fold(add, scores, rows), 0, keepdims=True)
+        total = jnp.sum(fold(add, scores, size), 0, keepdims=True)
         for piece in range(WIDE // LANES):
             at = chunk * (WIDE // LANES) + piece
             cut = slice(piece * LANES, (piece + 1) * LANES)
             tops[at : at + 1, :] = top[:, cut]
             totals[at : at + 1, :] = total[:, cut]
-
-
-def place(values, static, left_ref):
+        if after is not None:
+            after(chunk)
+
+
+def place(values, static, left_ref, first=0):
     blocks = values.shape[0]
     high = values.astype(bf16).astype(f32)
     rest = values - high
@@ -102,7 +103,7 @@
     lane = lax.broadcasted_iota(jnp.int32, (LANES, LANES), 1)
     owner = jnp.where(lane < LANES // 2, -1, wrap(lane, blocks))
     for block in range(blocks):
-        rows = pl.ds(block * LANES, LANES)
+        rows = pl.ds(first + block * LANES, LANES)
         added = jnp.where(owner == block, turned, 0.0).astype(bf16)
         left_ref[rows, LANES:] = static[rows, :] + added
 
@@ -135,10 +136,11 @@
     for peer in src_peers:
         pl.semaphore_signal(barrier, inc=1, device_id=(peer, my_tgt), device_id_type=MESH)
 
-    def row_copy(step, number):
+    def row_copy(step, half, number):
         return pltpu.make_async_remote_copy(
-            src_ref=row_out.at[step], dst_ref=row_in.at[step, number],
-            send_sem=row_send.at[step, number], recv_sem=row_recv.at[step, number],
+            src_ref=row_out.at[step, half], dst_ref=row_in.at[step, half, number],
+            send_sem=row_send.at[step, half, number],
+            recv_sem=row_recv.at[step, half, number],
             device_id=(my_src, tgt_peers[number]), device_id_type=MESH,
         )
 
@@ -227,30 +229,44 @@
     log_count = f32(math.log2(modulus))
     potential_g = -far
     buffers = (buffer_0, buffer_1)
+    share = blocks_i // HALVES
     for step in range(ITERS):
         place(weights + potential_g, b_static, b_left)
-        sweep(b_left, a_right, buffers, row_tops, row_totals)
-        row_out[step] = row_tops[...] + jnp.log(row_totals[...]) * f32(log2_e)
+
+        def send(chunk, step=step):
+            half, rest = divmod((chunk + 1) * WIDE, share * LANES)
+            if rest:
+                return
+            half = half - 1
+            cut = pl.ds(half * share, share)
+            row_out[step, half] = row_tops[cut, :] + jnp.log(row_totals[cut, :]) * f32(log2_e)
+            if step == 0 and half == 0:
+                pl.semaphore_wait(barrier, src - 1 + tgt - 1)
+            for number in range(tgt - 1):
+                row_copy(step, half, number).start()
+
+        sweep(b_left, a_right, buffers, (0, columns), row_tops, row_totals, send)
         if step == 0:
             peak = jnp.max(weights, keepdims=True)
             total = jnp.sum(jnp.exp2(weights - peak), keepdims=True)
             norm_out[...] = jnp.broadcast_to(
                 peak + jnp.log(total) * f32(log2_e), (8, LANES)
             )
-            pl.semaphore_wait(barrier, src - 1 + tgt - 1)
-        for number in range(tgt - 1):
-            row_copy(step, number).start()
-        if step == 0:
             for number in range(tgt - 1):
                 norm_copy(number).start()
-        for number in range(tgt - 1):
-            row_copy(step, number).wait_recv()
-        potential_f = -log_sum(
-            [row_out[step]] + [row_in[step, number] for number in range(tgt - 1)]
-        )
-        place(potential_f, a_static, a_left)
-        sweep(a_left, b_right, buffers, col_tops, col_totals)
-        col_out[step] = col_tops[...] + jnp.log(col_totals[...]) * f32(log2_e)
+        parts, potential_f = [], []
+        for half in range(HALVES):
+            for number in range(tgt - 1):
+                row_copy(step, half, number).wait_recv()
+            potential_f.append(-log_sum(
+                [row_out[step, half]]
+                + [row_in[step, half, number] for number in range(tgt - 1)]
+            ))
+            rows = (half * share * LANES, share * LANES)
+            place(potential_f[half], a_static, a_left, rows[0])
+            sweep(a_left, b_right, buffers, rows, col_tops, col_totals)
+            parts.append(col_tops[...] + jnp.log(col_totals[...]) * f32(log2_e))
+        col_out[step] = log_sum(parts)
         for number in range(src - 1):
             col_copy(step, number).start()
         if step == 0:
@@ -260,15 +276,20 @@
                 [norm_out[...]] + [norm_in[number] for number in range(tgt - 1)]
             )[0:1, :]
         if step == ITERS - 1:
-            out_ref[:blocks_i, :] = (potential_f + norm) * f32(1.0 / scale) + near_ref[...]
+            for half in range(HALVES):
+                cut = pl.ds(half * share, share)
+                out_ref[cut, :] = (
+                    (potential_f[half] + norm) * f32(1.0 / scale) + near_ref[cut, :]
+                )
         for number in range(src - 1):
             col_copy(step, number).wait_recv()
         sums = log_sum([col_out[step]] + [col_in[step, number] for number in range(src - 1)])
         potential_g = log_count - sums - norm
     out_ref[blocks_i:, :] = potential_g * f32(1.0 / scale) + far_ref[...]
     for step in range(ITERS):
-        for number in range(tgt - 1):
-            row_copy(step, number).wait_send()
+        for half in range(HALVES):
+            for number in range(tgt - 1):
+                row_copy(step, half, number).wait_send()
         for number in range(src - 1):
             col_copy(step, number).wait_send()
     for number in range(tgt - 1):
@@ -306,14 +327,14 @@
             pltpu.VMEM((blocks_i, LANES), f32),
             pltpu.VMEM((blocks_j, LANES), f32),
             pltpu.VMEM((blocks_j, LANES), f32),
-            pltpu.VMEM((ITERS, blocks_i, LANES), f32),
-            pltpu.VMEM((ITERS, tgt - 1, blocks_i, LANES), f32),
+            pltpu.VMEM((ITERS, HALVES, blocks_i // HALVES, LANES), f32),
+            pltpu.VMEM((ITERS, HALVES, tgt - 1, blocks_i // HALVES, LANES), f32),
             pltpu.VMEM((ITERS, blocks_j, LANES), f32),
             pltpu.VMEM((ITERS, src - 1, blocks_j, LANES), f32),
             pltpu.VMEM((8, LANES), f32),
             pltpu.VMEM((tgt - 1, 8, LANES), f32),
-            dma((ITERS, tgt - 1)),
-            dma((ITERS, tgt - 1)),
+            dma((ITERS, HALVES, tgt - 1)),
+            dma((ITERS, HALVES, tgt - 1)),
             dma((ITERS, src - 1)),
             dma((ITERS, src - 1)),
             dma((tgt - 1,)),

time: 30 us -> 29.3 us (0.977)
  Pallas kernels: 26.3 us -> 25.6 us
    pallas_call x1, Pallas kernels: 26.3 us -> 25.6 us  [local(): pl.pallas_call(functools.partial(kernel, sizes), out_shape=jax.ShapeDtype...]
where the time goes in v4:
time: 29.3 us; the launch traced here: 29.1 us
  Pallas kernels  25.6 us (87%)
  local copies, waits for them, and re-layouts  2.81 us (10%)
  between operations  0.67 us (2%)
    pallas_call x1, Pallas kernels, local(): pl.pallas_call(functools.partial(kernel, sizes), out_shape=jax.ShapeDtype...  25.6 us
    unnamed x8, local copies, waits for them, and re-layouts  1.62 us
    reshape x2, local copies, waits for them, and re-layouts, local(): return (both[:blocks_i].reshape(-1), both[blocks_i:].reshape(-1))  1.19 us

profile of v4, /device:TPU:0, one launch (start us, length us, event | category | flops | bytes accessed | tf_op | source)
XLA Modules:
  0.0 29.1 jit_solution(2230464713628403250)
XLA Ops:
  0.6 0.0 copy-start.1
  0.6 0.0 copy-start.2
  0.7 0.0 copy-start.3
  0.7 0.7 %copy-done.1 = f32[1024]{0:T(1024)S(1)} copy-done((f32[1024]{0:T(1024)S(1)}, f32[1024]{0:T(1024)}, u32[]{:S(2)}) %copy-start.1) | copy-done | bytes 4120
  1.3 0.0 copy-done.2
  1.3 0.0 copy-done.3
  1.3 0.0 copy-start
  1.3 0.9 %copy-done = f32[64,1024]{1,0:T(8,128)S(1)} copy-done((f32[64,1024]{1,0:T(8,128)S(1)}, f32[64,1024]{1,0:T(8,128)}, u32[]{:S(2)}) %copy-start) | copy-done | bytes 262168
  2.3 25.6 %shard_map.59 = f32[24,128]{1,0:T(8,128)S(1)} custom-call(s32[1,64]{1,0:T(1,128)S(1)} %bitcast.8, f32[1,64]{1,0:T(1,128)S(1)} %bitcast.9, f32[64,1024]{1,0:T(8,128)S(1)} %copy-done, f32[8,128]{1,0:T(8,128)S(1)} %bitcast.7), custom_call_target="tpu_custom_call" | custom-call | tf_op jit(solution)/shard_map/pallas_call | solution.py:305
  27.9 0.6 %slice_bitcast_fusion.1 = f32[1024]{0:T(1024)} fusion(f32[24,128]{1,0:T(8,128)S(1)} %shard_map.59), kind=kLoop, calls=%fused_computation.1 | loop fusion | bytes 8192 | tf_op jit(solution)/shard_map/reshape | solution.py:353
  28.5 0.6 %slice_bitcast_fusion = f32[2048]{0:T(1024)} fusion(f32[24,128]{1,0:T(8,128)S(1)} %shard_map.59), kind=kLoop, calls=%fused_computation | loop fusion | bytes 16384 | tf_op jit(solution)/shard_map/reshape | solution.py:353
Async XLA Ops:
  0.6 0.7 %copy-start.1 = (f32[1024]{0:T(1024)S(1)}, f32[1024]{0:T(1024)}, u32[]{:S(2)}) copy-start(f32[1024]{0:T(1024)} %param.7) | copy-start | bytes 12292
  0.6 0.7 %copy-start.2 = (s32[64]{0:T(128)S(1)}, s32[64]{0:T(128)}, u32[]{:S(2)}) copy-start(s32[64]{0:T(128)} %param.4) | copy-start | bytes 772
  0.7 0.7 %copy-start.3 = (f32[64]{0:T(128)S(1)}, f32[64]{0:T(128)}, u32[]{:S(2)}) copy-start(f32[64]{0:T(128)} %param.5) | copy-start | bytes 772
  1.3 1.0 %copy-start = (f32[64,1024]{1,0:T(8,128)S(1)}, f32[64,1024]{1,0:T(8,128)}, u32[]{:S(2)}) copy-start(f32[64,1024]{1,0:T(8,128)} %targets_hbm.1) | copy-start | bytes 786436

commit v5 on v4

--- a/solution.py
+++ b/solution.py
@@ -61,18 +61,23 @@
     count = right_ref.shape[1] // WIDE
 
     def product(chunk):
-        right = right_ref[:, pl.ds(chunk * WIDE, WIDE)]
-        buffers[chunk % 2][pl.ds(0, size), :] = jnp.dot(
-            left_ref[pl.ds(first, size), :], right, preferred_element_type=f32
-        )
-
-    product(0)
+        scores = jnp.dot(
+            left_ref[pl.ds(first, size), :],
+            right_ref[:, pl.ds(chunk * WIDE, WIDE)],
+            preferred_element_type=f32,
+        )
+        buffers[chunk % 2][pl.ds(0, size), :] = scores
+        running = scores[:TILE]
+        for start in range(TILE, size, TILE):
+            running = jnp.maximum(running, scores[start : start + TILE])
+        return jnp.max(running, 0, keepdims=True)
+
+    later = product(0)
     for chunk in range(count):
+        top = later
         if chunk + 1 < count:
-            product(chunk + 1)
+            later = product(chunk + 1)
         scores = buffers[chunk % 2]
-        top = fold(lambda a, b: b if a is None else jnp.maximum(a, b), scores, size)
-        top = jnp.max(top, 0, keepdims=True)
         shift = jnp.broadcast_to(top, (TILE, WIDE))
 
         def add(total, part):
@@ -99,37 +104,28 @@
     spare = LANES // 2 - 3 * blocks
     if spare:
         filler.append(jnp.zeros((spare, LANES), f32))
-    turned = jnp.concatenate(filler, 0).T
-    lane = lax.broadcasted_iota(jnp.int32, (LANES, LANES), 1)
+    turned = jnp.concatenate(filler, 0).T.astype(bf16)
+    lane = lax.broadcasted_iota(jnp.int32, (16, LANES), 1)
     owner = jnp.where(lane < LANES // 2, -1, wrap(lane, blocks))
     for block in range(blocks):
         rows = pl.ds(first + block * LANES, LANES)
-        added = jnp.where(owner == block, turned, 0.0).astype(bf16)
-        left_ref[rows, LANES:] = static[rows, :] + added
+        chosen = jnp.where(owner == block, 1.0, 0.0).astype(bf16)
+        chosen = jnp.concatenate([chosen] * (LANES // 16), 0)
+        left_ref[rows, LANES:] = static[rows, :] + turned * chosen
 
 
 def kernel(
-    sizes, generator_hbm, shift_hbm, targets_hbm, weights_hbm, out_ref,
-    generator_ref, shift_ref, targets_ref, weights_ref,
+    sizes, generator_ref, shift_ref, targets_ref, weights_ref, out_ref,
     a_left, a_right, a_static, b_left, b_right, b_static, buffer_0, buffer_1, pair, far_ref, near_ref,
     row_tops, row_totals, col_tops, col_totals,
     row_out, row_in, col_out, col_in, norm_out, norm_in,
-    row_send, row_recv, col_send, col_recv, norm_send, norm_recv, load,
+    row_send, row_recv, col_send, col_recv, norm_send, norm_recv,
 ):
     src, tgt = sizes
     modulus = SRC_DEV * src
     my_src, my_tgt = lax.axis_index("src"), lax.axis_index("tgt")
     src_peers = [lax.rem(my_src + step, src) for step in range(1, src)]
     tgt_peers = [lax.rem(my_tgt + step, tgt) for step in range(1, tgt)]
-    loads = [
-        pltpu.make_async_copy(source, place_in, load.at[number])
-        for number, (source, place_in) in enumerate((
-            (generator_hbm, generator_ref), (shift_hbm, shift_ref),
-            (targets_hbm, targets_ref), (weights_hbm, weights_ref),
-        ))
-    ]
-    for copy in loads:
-        copy.start()
     barrier = pltpu.get_barrier_semaphore()
     for peer in tgt_peers:
         pl.semaphore_signal(barrier, inc=1, device_id=(my_src, peer), device_id_type=MESH)
@@ -164,8 +160,6 @@
     lane = lax.broadcasted_iota(jnp.int32, (LANES, LANES), 1)
     first = lane < LANES // 2
 
-    loads[0].wait()
-    loads[1].wait()
     pair[0:1, : LANES // 2] = generator_ref[...].astype(f32)
     pair[1:2, : LANES // 2] = shift_ref[...]
     both = pair[0:2, :]
@@ -207,8 +201,6 @@
         a_right[2 * half : 3 * half, cut] = (points - high.astype(f32)).astype(bf16)
     a_right[3 * half :, :] = jnp.ones((half, SRC_DEV), bf16)
 
-    loads[2].wait()
-    loads[3].wait()
     for block in range(blocks_j):
         rows = pl.ds(block * LANES, LANES)
         part = targets_ref[:, block * LANES : (block + 1) * LANES]
@@ -275,6 +267,12 @@
             norm = log_sum(
                 [norm_out[...]] + [norm_in[number] for number in range(tgt - 1)]
             )[0:1, :]
+        for half in range(HALVES):
+            for number in range(tgt - 1):
+                row_copy(step, half, number).wait_send()
+        if step == 0:
+            for number in range(tgt - 1):
+                norm_copy(number).wait_send()
         if step == ITERS - 1:
             for half in range(HALVES):
                 cut = pl.ds(half * share, share)
@@ -282,18 +280,10 @@
                     (potential_f[half] + norm) * f32(1.0 / scale) + near_ref[cut, :]
                 )
         for number in range(src - 1):
-            col_copy(step, number).wait_recv()
+            col_copy(step, number).wait()
         sums = log_sum([col_out[step]] + [col_in[step, number] for number in range(src - 1)])
         potential_g = log_count - sums - norm
     out_ref[blocks_i:, :] = potential_g * f32(1.0 / scale) + far_ref[...]
-    for step in range(ITERS):
-        for half in range(HALVES):
-            for number in range(tgt - 1):
-                row_copy(step, half, number).wait_send()
-        for number in range(src - 1):
-            col_copy(step, number).wait_send()
-    for number in range(tgt - 1):
-        norm_copy(number).wait_send()
 
 
 def local(sizes, generator, shift, targets, log_weights):
@@ -305,13 +295,9 @@
     both = pl.pallas_call(
         functools.partial(kernel, sizes),
         out_shape=jax.ShapeDtypeStruct((blocks_i + blocks_j, LANES), f32),
-        in_specs=[pl.BlockSpec(memory_space=pltpu.HBM)] * 4,
+        in_specs=[vmem] * 4,
         out_specs=vmem,
         scratch_shapes=[
-            pltpu.VMEM((1, generator.shape[0]), jnp.int32),
-            pltpu.VMEM((1, shift.shape[0]), f32),
-            pltpu.VMEM(targets.shape, f32),
-            pltpu.VMEM((blocks_j, LANES), f32),
             pltpu.VMEM((SRC_DEV, 2 * LANES), bf16),
             pltpu.VMEM((2 * LANES, SRC_DEV), bf16),
             pltpu.VMEM((SRC_DEV, LANES), bf16),
@@ -339,7 +325,6 @@
             dma((ITERS, src - 1)),
             dma((tgt - 1,)),
             dma((tgt - 1,)),
-            dma((4,)),
         ],
         compiler_params=pltpu.CompilerParams(
             collective_id=0, has_side_effects=True, vmem_limit_bytes=LIMIT

time: 29.3 us -> 29.1 us (level)
  no operation moved by 1% of the time
where the time goes in v5:
time: 29.1 us; the launch traced here: 28.9 us
  Pallas kernels  25.5 us (88%)
  local copies, waits for them, and re-layouts  2.81 us (10%)
  between operations  0.67 us (2%)
    pallas_call x1, Pallas kernels, local(): pl.pallas_call(functools.partial(kernel, sizes), out_shape=jax.ShapeDtype...  25.5 us
    unnamed x8, local copies, waits for them, and re-layouts  1.62 us
    reshape x2, local copies, waits for them, and re-layouts, local(): return (both[:blocks_i].reshape(-1), both[blocks_i:].reshape(-1))  1.19 us

profile of v5, /device:TPU:0, one launch (start us, length us, event | category | flops | bytes accessed | tf_op | source)
XLA Modules:
  0.0 28.9 jit_solution(4904619477721898134)
XLA Ops:
  0.6 0.0 copy-start.1
  0.6 0.0 copy-start.2
  0.7 0.0 copy-start.3
  0.7 0.7 %copy-done.1 = f32[1024]{0:T(1024)S(1)} copy-done((f32[1024]{0:T(1024)S(1)}, f32[1024]{0:T(1024)}, u32[]{:S(2)}) %copy-start.1) | copy-done | bytes 4120
  1.3 0.0 copy-done.2
  1.3 0.0 copy-done.3
  1.3 0.0 copy-start
  1.3 0.9 %copy-done = f32[64,1024]{1,0:T(8,128)S(1)} copy-done((f32[64,1024]{1,0:T(8,128)S(1)}, f32[64,1024]{1,0:T(8,128)}, u32[]{:S(2)}) %copy-start) | copy-done | bytes 262168
  2.3 25.5 %shard_map.59 = f32[24,128]{1,0:T(8,128)S(1)} custom-call(s32[1,64]{1,0:T(1,128)S(1)} %bitcast.8, f32[1,64]{1,0:T(1,128)S(1)} %bitcast.9, f32[64,1024]{1,0:T(8,128)S(1)} %copy-done, f32[8,128]{1,0:T(8,128)S(1)} %bitcast.7), custom_call_target="tpu_custom_call" | custom-call | tf_op jit(solution)/shard_map/pallas_call | solution.py:295
  27.8 0.6 %slice_bitcast_fusion.1 = f32[1024]{0:T(1024)} fusion(f32[24,128]{1,0:T(8,128)S(1)} %shard_map.59), kind=kLoop, calls=%fused_computation.1 | loop fusion | bytes 8192 | tf_op jit(solution)/shard_map/reshape | solution.py:338
  28.3 0.6 %slice_bitcast_fusion = f32[2048]{0:T(1024)} fusion(f32[24,128]{1,0:T(8,128)S(1)} %shard_map.59), kind=kLoop, calls=%fused_computation | loop fusion | bytes 16384 | tf_op jit(solution)/shard_map/reshape | solution.py:338
Async XLA Ops:
  0.6 0.7 %copy-start.1 = (f32[1024]{0:T(1024)S(1)}, f32[1024]{0:T(1024)}, u32[]{:S(2)}) copy-start(f32[1024]{0:T(1024)} %param.7) | copy-start | bytes 12292
  0.6 0.7 %copy-start.2 = (s32[64]{0:T(128)S(1)}, s32[64]{0:T(128)}, u32[]{:S(2)}) copy-start(s32[64]{0:T(128)} %param.4) | copy-start | bytes 772
  0.7 0.7 %copy-start.3 = (f32[64]{0:T(128)S(1)}, f32[64]{0:T(128)}, u32[]{:S(2)}) copy-start(f32[64]{0:T(128)} %param.5) | copy-start | bytes 772
  1.3 1.0 %copy-start = (f32[64,1024]{1,0:T(8,128)S(1)}, f32[64,1024]{1,0:T(8,128)}, u32[]{:S(2)}) copy-start(f32[64,1024]{1,0:T(8,128)} %targets_ref.1) | copy-start | bytes 786436

commit v6 on v5

--- a/solution.py
+++ b/solution.py
@@ -176,23 +176,15 @@
         wrap(outer * generator, modulus).astype(f32) / modulus + shift
     )
     half = LANES // 2
-    for block in range(blocks_i):
-        rows = pl.ds(block * LANES, LANES)
-        points = (
-            sin_out[block : block + 1, :] * cos_in + cos_out[block : block + 1, :] * sin_in
-        )
-        high = points.astype(bf16)
-        a_left[rows, :LANES] = high
-        a_static[rows, :] = jnp.where(first, points - high.astype(f32), 0.0).astype(bf16)
-    sin_in, cos_in = sin_in.T[:half, :], cos_in.T[:half, :]
+    sin_turned, cos_turned = sin_in.T[:half, :], cos_in.T[:half, :]
     outside = jnp.concatenate(
         [sin_out, cos_out, jnp.zeros((LANES - 2 * blocks_i, LANES), f32)], 0
     ).T[:half, :]
     for block in range(blocks_i):
         cut = pl.ds(block * LANES, LANES)
         points = (
-            outside[:, block : block + 1] * cos_in
-            + outside[:, blocks_i + block : blocks_i + block + 1] * sin_in
+            outside[:, block : block + 1] * cos_turned
+            + outside[:, blocks_i + block : blocks_i + block + 1] * sin_turned
         )
         near_ref[block : block + 1, :] = 0.5 * jnp.sum(points * points, 0, keepdims=True)
         high = points.astype(bf16)
@@ -211,10 +203,25 @@
         turned = jnp.concatenate([high.astype(f32), low], 0).T
         b_left[rows, :LANES] = turned.astype(bf16)
         b_static[rows, :] = jnp.where(first, turned, 0.0).astype(bf16)
-        b_right[:half, rows] = high
-        b_right[half : 2 * half, rows] = low.astype(bf16)
-        b_right[2 * half : 3 * half, rows] = high
-    b_right[3 * half :, :] = jnp.ones((half, columns), bf16)
+
+    def prepare():
+        for block in range(blocks_i):
+            rows = pl.ds(block * LANES, LANES)
+            points = (
+                sin_out[block : block + 1, :] * cos_in
+                + cos_out[block : block + 1, :] * sin_in
+            )
+            high = points.astype(bf16)
+            a_left[rows, :LANES] = high
+            a_static[rows, :] = jnp.where(first, points - high.astype(f32), 0.0).astype(bf16)
+        for block in range(blocks_j):
+            cut = pl.ds(block * LANES, LANES)
+            part = targets_ref[:, block * LANES : (block + 1) * LANES] * f32(scale)
+            high = part.astype(bf16)
+            b_right[:half, cut] = high
+            b_right[half : 2 * half, cut] = (part - high.astype(f32)).astype(bf16)
+            b_right[2 * half : 3 * half, cut] = high
+        b_right[3 * half :, :] = jnp.ones((half, columns), bf16)
 
     weights = weights_ref[...] * f32(log2_e)
     far = far_ref[...] * f32(scale)
@@ -246,6 +253,7 @@
             )
             for number in range(tgt - 1):
                 norm_copy(number).start()
+            prepare()
         parts, potential_f = [], []
         for half in range(HALVES):
             for number in range(tgt - 1):

time: 29.1 us -> 29.2 us (level)
  no operation moved by 1% of the time
where the time goes in v6:
time: 29.2 us; the launch traced here: 29 us
  Pallas kernels  25.5 us (87%)
  local copies, waits for them, and re-layouts  2.81 us (10%)
  between operations  0.67 us (2%)
    pallas_call x1, Pallas kernels, local(): pl.pallas_call(functools.partial(kernel, sizes), out_shape=jax.ShapeDtype...  25.5 us
    unnamed x8, local copies, waits for them, and re-layouts  1.62 us
    reshape x2, local copies, waits for them, and re-layouts, local(): return (both[:blocks_i].reshape(-1), both[blocks_i:].reshape(-1))  1.19 us

profile of v6, /device:TPU:0, one launch (start us, length us, event | category | flops | bytes accessed | tf_op | source)
XLA Modules:
  0.0 29.0 jit_solution(4540125277998712181)
XLA Ops:
  0.6 0.0 copy-start.1
  0.6 0.0 copy-start.2
  0.7 0.0 copy-start.3
  0.7 0.7 %copy-done.1 = f32[1024]{0:T(1024)S(1)} copy-done((f32[1024]{0:T(1024)S(1)}, f32[1024]{0:T(1024)}, u32[]{:S(2)}) %copy-start.1) | copy-done | bytes 4120
  1.3 0.0 copy-done.2
  1.3 0.0 copy-done.3
  1.3 0.0 copy-start
  1.3 0.9 %copy-done = f32[64,1024]{1,0:T(8,128)S(1)} copy-done((f32[64,1024]{1,0:T(8,128)S(1)}, f32[64,1024]{1,0:T(8,128)}, u32[]{:S(2)}) %copy-start) | copy-done | bytes 262168
  2.3 25.5 %shard_map.59 = f32[24,128]{1,0:T(8,128)S(1)} custom-call(s32[1,64]{1,0:T(1,128)S(1)} %bitcast.8, f32[1,64]{1,0:T(1,128)S(1)} %bitcast.9, f32[64,1024]{1,0:T(8,128)S(1)} %copy-done, f32[8,128]{1,0:T(8,128)S(1)} %bitcast.7), custom_call_target="tpu_custom_call" | custom-call | tf_op jit(solution)/shard_map/pallas_call | solution.py:303
  27.8 0.6 %slice_bitcast_fusion.1 = f32[1024]{0:T(1024)} fusion(f32[24,128]{1,0:T(8,128)S(1)} %shard_map.59), kind=kLoop, calls=%fused_computation.1 | loop fusion | bytes 8192 | tf_op jit(solution)/shard_map/reshape | solution.py:346
  28.4 0.6 %slice_bitcast_fusion = f32[2048]{0:T(1024)} fusion(f32[24,128]{1,0:T(8,128)S(1)} %shard_map.59), kind=kLoop, calls=%fused_computation | loop fusion | bytes 16384 | tf_op jit(solution)/shard_map/reshape | solution.py:346
Async XLA Ops:
  0.6 0.7 %copy-start.1 = (f32[1024]{0:T(1024)S(1)}, f32[1024]{0:T(1024)}, u32[]{:S(2)}) copy-start(f32[1024]{0:T(1024)} %param.7) | copy-start | bytes 12292
  0.6 0.7 %copy-start.2 = (s32[64]{0:T(128)S(1)}, s32[64]{0:T(128)}, u32[]{:S(2)}) copy-start(s32[64]{0:T(128)} %param.4) | copy-start | bytes 772
  0.7 0.7 %copy-start.3 = (f32[64]{0:T(128)S(1)}, f32[64]{0:T(128)}, u32[]{:S(2)}) copy-start(f32[64]{0:T(128)} %param.5) | copy-start | bytes 772
  1.3 1.0 %copy-start = (f32[64,1024]{1,0:T(8,128)S(1)}, f32[64,1024]{1,0:T(8,128)}, u32[]{:S(2)}) copy-start(f32[64,1024]{1,0:T(8,128)} %targets_ref.1) | copy-start | bytes 786436

commit v7 on v6

--- a/solution.py
+++ b/solution.py
@@ -13,7 +13,7 @@
 LANES = 128
 WIDE = 256
 TILE = 64
-LIMIT = 40 * 2**20
+LIMIT = 54 * 2**20 - 2**17
 HALVES = 2
 
 blur_level = 0.1
@@ -115,17 +115,19 @@
 
 
 def kernel(
-    sizes, generator_ref, shift_ref, targets_ref, weights_ref, out_ref,
+    sizes, generator_ref, shift_ref, targets_hbm, weights_ref, out_ref, targets_ref,
     a_left, a_right, a_static, b_left, b_right, b_static, buffer_0, buffer_1, pair, far_ref, near_ref,
     row_tops, row_totals, col_tops, col_totals,
     row_out, row_in, col_out, col_in, norm_out, norm_in,
-    row_send, row_recv, col_send, col_recv, norm_send, norm_recv,
+    row_send, row_recv, col_send, col_recv, norm_send, norm_recv, load,
 ):
     src, tgt = sizes
     modulus = SRC_DEV * src
     my_src, my_tgt = lax.axis_index("src"), lax.axis_index("tgt")
     src_peers = [lax.rem(my_src + step, src) for step in range(1, src)]
     tgt_peers = [lax.rem(my_tgt + step, tgt) for step in range(1, tgt)]
+    fetch = pltpu.make_async_copy(targets_hbm, targets_ref, load)
+    fetch.start()
     barrier = pltpu.get_barrier_semaphore()
     for peer in tgt_peers:
         pl.semaphore_signal(barrier, inc=1, device_id=(my_src, peer), device_id_type=MESH)
@@ -193,6 +195,7 @@
         a_right[2 * half : 3 * half, cut] = (points - high.astype(f32)).astype(bf16)
     a_right[3 * half :, :] = jnp.ones((half, SRC_DEV), bf16)
 
+    fetch.wait()
     for block in range(blocks_j):
         rows = pl.ds(block * LANES, LANES)
         part = targets_ref[:, block * LANES : (block + 1) * LANES]
@@ -303,9 +306,10 @@
     both = pl.pallas_call(
         functools.partial(kernel, sizes),
         out_shape=jax.ShapeDtypeStruct((blocks_i + blocks_j, LANES), f32),
-        in_specs=[vmem] * 4,
+        in_specs=[vmem, vmem, pl.BlockSpec(memory_space=pltpu.HBM), vmem],
         out_specs=vmem,
         scratch_shapes=[
+            pltpu.VMEM(targets.shape, f32),
             pltpu.VMEM((SRC_DEV, 2 * LANES), bf16),
             pltpu.VMEM((2 * LANES, SRC_DEV), bf16),
             pltpu.VMEM((SRC_DEV, LANES), bf16),
@@ -333,6 +337,7 @@
             dma((ITERS, src - 1)),
             dma((tgt - 1,)),
             dma((tgt - 1,)),
+            dma,
         ],
         compiler_params=pltpu.CompilerParams(
             collective_id=0, has_side_effects=True, vmem_limit_bytes=LIMIT

time: 29.2 us -> 28.2 us (0.966)
  local copies, waits for them, and re-layouts: 2.81 us -> 1.86 us
    unnamed x8 -> x6, local copies, waits for them, and re-layouts: 1.62 us -> 0.67 us
where the time goes in v7:
time: 28.2 us; the launch traced here: 28 us
  Pallas kernels  25.5 us (90%)
  local copies, waits for them, and re-layouts  1.86 us (7%)
  between operations  0.66 us (2%)
    pallas_call x1, Pallas kernels, local(): pl.pallas_call(functools.partial(kernel, sizes), out_shape=jax.ShapeDtype...  25.5 us
    reshape x2, local copies, waits for them, and re-layouts, local(): return (both[:blocks_i].reshape(-1), both[blocks_i:].reshape(-1))  1.19 us
    unnamed x6, local copies, waits for them, and re-layouts  0.67 us

profile of v7, /device:TPU:0, one launch (start us, length us, event | category | flops | bytes accessed | tf_op | source)
XLA Modules:
  0.0 28.0 jit_solution(17523175005004440598)
XLA Ops:
  0.6 0.0 copy-start
  0.6 0.0 copy-start.1
  0.7 0.0 copy-start.2
  0.7 0.7 %copy-done = f32[1024]{0:T(1024)S(1)} copy-done((f32[1024]{0:T(1024)S(1)}, f32[1024]{0:T(1024)}, u32[]{:S(2)}) %copy-start) | copy-done | bytes 4120
  1.3 0.0 copy-done.1
  1.3 0.0 copy-done.2
  1.3 25.5 %shard_map.59 = f32[24,128]{1,0:T(8,128)S(1)} custom-call(s32[1,64]{1,0:T(1,128)S(1)} %bitcast.8, f32[1,64]{1,0:T(1,128)S(1)} %bitcast.9, f32[64,1024]{1,0:T(8,128)} %targets_hbm.1, f32[8,128]{1,0:T(8,128)S(1)} %bitcast.7), custom_call_target="tpu_custom_call" | custom-call | tf_op jit(solution)/shard_map/pallas_call | solution.py:306
  26.8 0.6 %slice_bitcast_fusion.1 = f32[1024]{0:T(1024)} fusion(f32[24,128]{1,0:T(8,128)S(1)} %shard_map.59), kind=kLoop, calls=%fused_computation.1 | loop fusion | bytes 8192 | tf_op jit(solution)/shard_map/reshape | solution.py:351
  27.4 0.6 %slice_bitcast_fusion = f32[2048]{0:T(1024)} fusion(f32[24,128]{1,0:T(8,128)S(1)} %shard_map.59), kind=kLoop, calls=%fused_computation | loop fusion | bytes 16384 | tf_op jit(solution)/shard_map/reshape | solution.py:351
Async XLA Ops:
  0.6 0.7 %copy-start = (f32[1024]{0:T(1024)S(1)}, f32[1024]{0:T(1024)}, u32[]{:S(2)}) copy-start(f32[1024]{0:T(1024)} %param.7) | copy-start | bytes 12292
  0.6 0.7 %copy-start.1 = (s32[64]{0:T(128)S(1)}, s32[64]{0:T(128)}, u32[]{:S(2)}) copy-start(s32[64]{0:T(128)} %param.4) | copy-start | bytes 772
  0.7 0.7 %copy-start.2 = (f32[64]{0:T(128)S(1)}, f32[64]{0:T(128)}, u32[]{:S(2)}) copy-start(f32[64]{0:T(128)} %param.5) | copy-start | bytes 772
